TPU v7x, 32 devices: a whole 2x2x4 slice. The times are simulated.
32 devices in a mesh: section: 2 (over y), expert: 4 (over z), dp: 4 (over x, core).
Axes of the slice: x: 2, y: 2, z: 4, core: 2. Of those that a mesh axis runs over, the one named last changes fastest.
Arguments:
- inputs: bfloat16 [2, 128, 3072], P(None, ('expert', 'dp')), may hold values from -6 to 6
- cotangent: bfloat16 [2, 128, 3072], P(None, ('expert', 'dp')), may hold values from -6 to 6
- norm_gain: bfloat16 [2, 3072], P('section'), may hold values from 0.5 to 1.5
- router: bfloat16 [2, 3072, 4], P('section'), may hold values from -0.109375 to 0.109375
- w_gate: bfloat16 [2, 4, 3072, 8192], P('section', 'expert', None, 'dp'), may hold values from -0.109375 to 0.109375
- w_up: bfloat16 [2, 4, 3072, 8192], P('section', 'expert', None, 'dp'), may hold values from -0.109375 to 0.109375
- w_down: bfloat16 [2, 4, 8192, 3072], P('section', 'expert', 'dp'), may hold values from -0.0625 to 0.0625
- routes: int32 [2, 2, 128, 2], P('section', None, ('expert', 'dp')), may hold values from 0 to 3, as said below
Outputs:
- acts: bfloat16 [2, 2, 128, 3072], P('section', None, ('expert', 'dp'))
- grads: bfloat16 [2, 2, 128, 3072], P('section', None, ('expert', 'dp'))
- router_grad: float32 [2, 3072, 4], P('section')
Inputs may be any that keep to these rules, and one draw needn't show every extreme that they name: `routes`: the two experts of a token differ. For each layer and micro-batch, the 8 tokens of one device name no expert more than 6 times, and one expert, the same on all devices for that layer and micro-batch, exactly 6 times.
All inputs are finite; a program needn't handle non-finite values.
Results may differ from a plain program's by a relative error of at most 0.017.
Values may be sent and summed in bfloat16 or wider, within the bound.
No kernel may reach another device: no remote copies, remote signals or barrier semaphores. Data moves between devices by JAX's collectives and lax.ppermute only.
A program may use at most 128 MiB of HBM per device.

v0:
```python
import functools

import jax
import jax.numpy as jnp
from jax import lax
from jax.experimental import pallas as pl
from jax.experimental.pallas import tpu as pltpu
from jax.sharding import PartitionSpec as P

EPSILON = 1e-05
LANES = 128
GROUP = ("expert", "dp")
F32 = jnp.float32
BF16 = jnp.bfloat16


def dot_nn(a, b):
    return jnp.dot(a, b, preferred_element_type=F32)


def dot_nt(a, b):
    return lax.dot_general(a, b, (((1,), (1,)), ((), ())), preferred_element_type=F32)


def lanes_like(rows):
    return lax.broadcasted_iota(jnp.int32, (rows, LANES), 1)


def pick_lane(block, lane):
    return jnp.sum(jnp.where(lanes_like(block.shape[0]) == lane, block, 0.0), axis=1, keepdims=True)


def hi_lo(block):
    high = block.astype(BF16)
    return high, (block - high.astype(F32)).astype(BF16)


def place_rows(tail, me, place_ref, pick_ref):
    tokens, rows = place_ref.shape
    wide = -(-rows // LANES) * LANES
    first, second = pick_lane(tail, 0), pick_lane(tail, 1)
    mine = jnp.broadcast_to(((first == me) | (second == me)).astype(F32), (tokens, wide))
    row = lax.broadcasted_iota(jnp.int32, (tokens, tokens), 0)
    col = lax.broadcasted_iota(jnp.int32, (tokens, tokens), 1)
    earlier = dot_nn((col < row).astype(F32).astype(BF16), mine.astype(BF16))
    slot = lax.broadcasted_iota(jnp.int32, (tokens, wide), 1).astype(F32)
    place = jnp.where((earlier == slot) & (mine > 0.5), 1.0, 0.0)
    place_ref[...] = place[:, :rows].astype(BF16)
    pick_ref[...] = jnp.transpose(place)[:rows].astype(BF16)


def signs_of(tail, me):
    first, second = pick_lane(tail, 0), pick_lane(tail, 1)
    other = first + second - me
    lane = lanes_like(tail.shape[0]).astype(F32)
    both = (lane == me).astype(F32) - (lane == other).astype(F32)
    return jnp.where(first != second, both, 0.0)


def norm_and_gap(rows_ref, router_ref, signs, hidden_ref):
    rows, width = rows_ref.shape

    def square(i, part, total):
        values = rows_ref[:, part].astype(F32)
        return total + jnp.sum(values * values, axis=1, keepdims=True)

    squares = tiles(width, square, jnp.zeros((rows, 1), F32))
    inv_rms = lax.rsqrt(squares / width + EPSILON)

    def scale(i, part, total):
        hidden = (rows_ref[:, part].astype(F32) * inv_rms * router_ref[LANES - 1:, part].astype(F32)).astype(BF16)
        hidden_ref[:, part] = hidden
        return total + dot_nt(hidden, router_ref[:, part])

    logits = tiles(width, scale, jnp.zeros((rows, LANES), F32))
    return jnp.sum(logits * signs, axis=1, keepdims=True)


def tile_of(total, most=1024):
    return next(c for c in (1024, 512, 256, 128) if c <= most and total % c == 0)


def tiles(total, body, carry=0, most=1024):
    step = tile_of(total, most)

    def one(i, carry):
        return body(i, pl.ds(pl.multiple_of(i * step, step), step), carry)

    return lax.fori_loop(0, total // step, one, carry)


class Loads:
    def __init__(self, source, target, sems, axis):
        self.source, self.target, self.sems, self.axis = source, target, sems, axis
        self.count, self.total = sems.shape[0], target.shape[axis]

    def copy(self, i):
        step = self.total // self.count
        part = pl.ds(pl.multiple_of(i * step, step), step)
        spot = (slice(None), part) if self.axis else (part,)
        return pltpu.make_async_copy(self.source.at[spot], self.target.at[spot], self.sems.at[i])

    def wait(self, i):
        self.copy(i).wait()


def start_all(*loads):
    def one(i, carry):
        for load in loads:
            load.copy(i).start()
        return carry

    lax.fori_loop(0, loads[0].count, one, 0)


def select(pick_ref, x_ref, rows_ref):
    def body(i, part, carry):
        rows_ref[:, part] = dot_nn(pick_ref[...], x_ref[:, part]).astype(BF16)
        return carry

    tiles(rows_ref.shape[1], body)


def piece_copies(x_refs, x_ref, sems):
    start, copies = 0, []
    for i, ref in enumerate(x_refs):
        copies.append(pltpu.make_async_copy(ref, x_ref.at[pl.ds(start, ref.shape[0])], sems.at[i]))
        start += ref.shape[0]
    return copies


def fetch(x_refs, x_ref, sems):
    copies = piece_copies(x_refs, x_ref, sems)
    for copy in copies:
        copy.start()
    for copy in copies:
        copy.wait()


def spread(place_ref, rows, out_refs, part):
    piece = out_refs[0].shape[0]
    block = dot_nn(place_ref[...], rows).astype(BF16)
    for i, out_ref in enumerate(out_refs):
        out_ref[:, part] = block[i * piece:(i + 1) * piece]


def send_down(active_ref, down_ref, down_loads, prob, place_ref, out_refs):
    def body(i, part, carry):
        down_loads.wait(i)
        rows = dot_nn(active_ref[...], down_ref[:, part]) * prob
        spread(place_ref, rows.astype(BF16), out_refs, part)
        return carry

    tiles(down_ref.shape[1], body)


def grads_of(gate_pre, up_pre, d_raw, prob, part, dprob_ref, active_ref, d_gate_ref, d_up_ref):
    gate_sig = jax.nn.sigmoid(gate_pre)
    act = gate_pre * gate_sig
    active = (act * up_pre).astype(BF16)
    if active_ref is not None:
        active_ref[:, part] = active
    gain = jnp.sum(active.astype(F32) * d_raw, axis=1, keepdims=True)
    dprob_ref[...] += jnp.broadcast_to(gain, dprob_ref.shape)
    d_active = d_raw * prob
    d_gate = d_active * up_pre * gate_sig * (1.0 + gate_pre * (1.0 - gate_sig))
    d_gate_ref[:, part] = d_gate.astype(BF16)
    d_up_ref[:, part] = (d_active * act).astype(BF16)


def turn_around(loads, source, target, stores, earlier):
    width = source.shape[0]
    step = tile_of(width)

    def body(i, part, carry):
        loads.wait(i)
        if earlier is not None:
            earlier.wait(i)
        for start in range(0, width, step):
            cols = pl.ds(start, step)
            target[part, cols] = jnp.transpose(source[cols, part])
        stores.copy(i).start()
        return carry

    tiles(source.shape[1], body, most=512)


def send_back(gate_ref, up_ref, gate_loads, up_loads, d_gate_ref, d_up_ref, dprob_ref, gap, signs,
              hidden_ref, router_ref, place_ref, out_refs, rg_ref):
    c = jax.nn.sigmoid(gap) * jax.nn.sigmoid(-gap) * dprob_ref[...] * signs
    c_high, c_low = hi_lo(c)
    t_high, t_low = hi_lo(jnp.transpose(c)[:rg_ref.shape[0]])

    def body(i, part, carry):
        if gate_loads is not None:
            gate_loads.wait(i)
            up_loads.wait(i)
        if gate_loads is not None:
            back = dot_nn(d_gate_ref[...], gate_ref[:, part]) + dot_nn(d_up_ref[...], up_ref[:, part])
        else:
            back = dot_nt(d_gate_ref[...], gate_ref[part, :]) + dot_nt(d_up_ref[...], up_ref[part, :])
        extra = dot_nn(c_high, router_ref[:, part]) + dot_nn(c_low, router_ref[:, part])
        spread(place_ref, (back + extra).astype(BF16), out_refs, part)
        hidden = hidden_ref[:, part]
        rg_ref[:, part] = dot_nn(t_high, hidden) + dot_nn(t_low, hidden)
        return carry

    tiles(router_ref.shape[1], body)


def first_kernel(x_refs, out_refs, router_ref, gate_in, up_in, down_in,
                 place_ref, pick_ref, hidden_ref, info_ref, a_ref, b_ref,
                 x_ref, x_sems, gate_ref, up_ref, down_ref, gate_sems, up_sems, rows_sems, cols_sems,
                 rows_ref, active_ref):
    section = lax.axis_index("section")
    width = router_ref.shape[1]
    gate_loads = Loads(gate_in, gate_ref, gate_sems, 1)
    up_loads = Loads(up_in, up_ref, up_sems, 1)
    down_cols = Loads(down_in, down_ref, cols_sems, 1)
    down_rows = Loads(down_in, down_ref, rows_sems, 0)
    fetches = piece_copies(x_refs, x_ref, x_sems)
    for copy in fetches:
        copy.start()

    @pl.when(section == 0)
    def _():
        start_all(gate_loads, up_loads)
        start_all(down_cols)

    @pl.when(section != 0)
    def _():
        start_all(down_rows)

    for copy in fetches:
        copy.wait()
    me = lax.axis_index("expert").astype(F32)
    tail = x_ref[:, width:]
    place_rows(tail.astype(F32), me, place_ref, pick_ref)
    select(pick_ref, x_ref, rows_ref)
    info_ref[0] = signs_of(dot_nn(pick_ref[...], tail), me)

    @pl.when(section == 0)
    def _():
        gap = norm_and_gap(rows_ref, router_ref, info_ref[0], hidden_ref)
        info_ref[1] = jnp.broadcast_to(gap, info_ref.shape[1:])

        def body(i, part, carry):
            gate_loads.wait(i)
            up_loads.wait(i)
            gate_pre = dot_nn(hidden_ref[...], gate_ref[:, part])
            up_pre = dot_nn(hidden_ref[...], up_ref[:, part])
            a_ref[:, part] = gate_pre.astype(BF16)
            b_ref[:, part] = up_pre.astype(BF16)
            active_ref[:, part] = (gate_pre * jax.nn.sigmoid(gate_pre) * up_pre).astype(BF16)
            return carry

        tiles(gate_ref.shape[1], body, most=512)
        send_down(active_ref, down_ref, down_cols, jax.nn.sigmoid(gap), place_ref, out_refs)

    @pl.when(section != 0)
    def _():
        def body(i, part, carry):
            down_rows.wait(i)
            a_ref[:, part] = dot_nt(rows_ref[...], down_ref[part, :]).astype(BF16)
            return carry

        tiles(down_ref.shape[0], body)


def middle_kernel(x_refs, back_refs, router_ref, place_ref, pick_ref, info_ref, raw_ref,
                  gate_in, up_in, down_in,
                  active_ref, prob_ref, rg_ref, gate_out, up_out,
                  x_ref, x_sems, gate_ref, up_ref, down_ref, gate_sems, up_sems, rows_sems, cols_sems,
                  rows_ref, hidden_ref, d_gate_ref, d_up_ref, dprob_ref, store_sems):
    section = lax.axis_index("section")

    @pl.when(section == 0)
    def _():
        gate_loads = Loads(gate_in, gate_ref, gate_sems, 1)
        up_loads = Loads(up_in, up_ref, up_sems, 1)
        start_all(gate_loads, up_loads)
        gate_stores = Loads(down_ref, gate_out, store_sems, 0)
        up_stores = Loads(down_ref, up_out, store_sems, 0)
        turn_around(gate_loads, gate_ref, down_ref, gate_stores, None)
        turn_around(up_loads, up_ref, down_ref, up_stores, gate_stores)
        lax.fori_loop(0, up_stores.count, lambda i, carry: (up_stores.wait(i), carry)[1], 0)

    @pl.when(section == 1)
    def _():
        gate_loads = Loads(gate_in, gate_ref, gate_sems, 1)
        up_loads = Loads(up_in, up_ref, up_sems, 1)
        fetches = piece_copies(x_refs, x_ref, x_sems)
        for copy in fetches:
            copy.start()
        start_all(gate_loads, up_loads)
        for copy in fetches:
            copy.wait()
        select(pick_ref, x_ref, rows_ref)
        signs = info_ref[0]
        gap = norm_and_gap(rows_ref, router_ref, signs, hidden_ref)
        prob = jax.nn.sigmoid(gap)
        prob_ref[...] = jnp.broadcast_to(prob, prob_ref.shape)
        dprob_ref[...] = jnp.zeros_like(dprob_ref)

        def body(i, part, carry):
            gate_loads.wait(i)
            up_loads.wait(i)
            gate_pre = dot_nn(hidden_ref[...], gate_ref[:, part])
            up_pre = dot_nn(hidden_ref[...], up_ref[:, part])
            grads_of(gate_pre, up_pre, raw_ref[:, part].astype(F32), prob, part, dprob_ref,
                     active_ref, d_gate_ref, d_up_ref)
            return carry

        tiles(gate_ref.shape[1], body, most=512)
        send_back(gate_ref, up_ref, None, None, d_gate_ref, d_up_ref, dprob_ref, gap, signs,
                  hidden_ref, router_ref, place_ref, back_refs, rg_ref)


def last_kernel(u_refs, out_refs, router_ref, place_ref, pick_ref, info_ref, hidden_ref, prob_ref,
                rg_in_ref, a_ref, b_ref, active_ref, gate_in, up_in, down_in,
                rg_ref,
                x_ref, x_sems, gate_ref, up_ref, down_ref, gate_sems, up_sems, rows_sems, cols_sems,
                rows_ref, d_gate_ref, d_up_ref, dprob_ref):
    section = lax.axis_index("section")

    @pl.when(section == 0)
    def _():
        down_rows = Loads(down_in, down_ref, rows_sems, 0)
        gate_loads = Loads(gate_in, gate_ref, gate_sems, 1)
        up_loads = Loads(up_in, up_ref, up_sems, 1)
        fetches = piece_copies(u_refs, x_ref, x_sems)
        for copy in fetches:
            copy.start()
        start_all(down_rows)
        start_all(gate_loads, up_loads)
        for copy in fetches:
            copy.wait()
        select(pick_ref, x_ref, rows_ref)
        gap = pick_lane(info_ref[1], 0)
        prob = jax.nn.sigmoid(gap)
        dprob_ref[...] = jnp.zeros_like(dprob_ref)

        def body(i, part, carry):
            down_rows.wait(i)
            d_raw = dot_nt(rows_ref[...], down_ref[part, :])
            grads_of(a_ref[:, part].astype(F32), b_ref[:, part].astype(F32), d_raw, prob, part,
                     dprob_ref, None, d_gate_ref, d_up_ref)
            return carry

        tiles(down_ref.shape[0], body)
        send_back(gate_ref, up_ref, gate_loads, up_loads, d_gate_ref, d_up_ref, dprob_ref, gap,
                  info_ref[0], hidden_ref, router_ref, place_ref, out_refs, rg_ref)

    @pl.when(section != 0)
    def _():
        down_cols = Loads(down_in, down_ref, cols_sems, 1)
        start_all(down_cols)
        send_down(active_ref, down_ref, down_cols, pick_lane(prob_ref[...], 0), place_ref, out_refs)
        rg_ref[...] = rg_in_ref[...]


def with_pieces(body, count, inputs, groups, *refs):
    ins, rest = refs[:inputs], refs[inputs:]
    body(ins[:count], rest[:groups], *ins[count:], *rest[groups:])


def expert_call(body, pieces, small, weights, outs, scratch, flops, far=(), by_rows=False):
    hidden_units, width = weights[2].shape
    shape = jax.ShapeDtypeStruct
    groups = lax.axis_size("dp")
    tokens = sum(p.shape[0] for p in pieces)
    outs = [shape((tokens // groups, width), BF16)] * groups + outs
    sems = lambda total, most: pltpu.SemaphoreType.DMA((total // tile_of(total, most),))
    pair = sems(width, 1024) if by_rows else sems(hidden_units, 512)
    scratch = [
        pltpu.VMEM((tokens, pieces[0].shape[1]), BF16), pltpu.SemaphoreType.DMA((len(pieces),)),
        *[pltpu.VMEM(w.shape, BF16) for w in weights],
        pair, pair, sems(hidden_units, 1024), sems(width, 1024),
    ] + scratch
    held = sum(w.size * w.dtype.itemsize for w in weights)
    block, outside = pl.BlockSpec(memory_space=pltpu.VMEM), pl.BlockSpec(memory_space=pl.ANY)
    in_specs = [outside] * len(pieces) + [block] * len(small) + [outside] * len(weights)
    results = pl.pallas_call(
        functools.partial(with_pieces, body, len(pieces), len(in_specs), groups),
        in_specs=in_specs,
        out_specs=[block] * len(outs) + [outside] * len(far),
        out_shape=outs + list(far),
        scratch_shapes=scratch,
        cost_estimate=pl.CostEstimate(flops=flops, bytes_accessed=held, transcendentals=0),
        compiler_params=pltpu.CompilerParams(
            vmem_limit_bytes=held + 6 * 2**20 + 4 * tokens * width * 2
        ),
    )(*pieces, *small, *weights)
    return results[:groups], *results[groups:]


def moved(block, axes, target):
    sizes = [lax.axis_size(a) for a in axes]
    spots = [()]
    for n in sizes:
        spots = [spot + (i,) for spot in spots for i in range(n)]
    number = {spot: i for i, spot in enumerate(spots)}
    pairs = [(number[spot], number[target(*spot)]) for spot in spots if target(*spot) in number]
    return lax.ppermute(block, axes, pairs)


def flips():
    bits = lax.axis_size("dp").bit_length() - 1
    return [1 << b for b in reversed(range(bits))]


def flipped(block, bit):
    return moved(block, ("dp",), lambda d: (d ^ bit,))


def gathered(block):
    count = lax.axis_size("expert")
    parts = [block] + [
        moved(block, ("expert",), lambda e, k=k: ((e + k) % count,)) for k in range(1, count)
    ]
    groups = [parts]
    for bit in flips():
        ahead = groups
        if bit == flips()[-1] and len(groups) > 1:
            ahead = [lax.optimization_barrier((parts, groups[1][-1]))[0]] + groups[1:]
        groups = groups + [[flipped(part, bit) for part in group] for group in ahead]
    return [part for group in groups for part in group]


def combined(pieces, hop=0, late=None):
    count = lax.axis_size("expert")
    own = pieces[0].shape[0] // count
    add = lambda kept, came: (kept.astype(F32) + came.astype(F32)).astype(BF16)
    cut = lambda group: [group[k * own:(k + 1) * own] for k in range(count)]
    order = list(reversed(flips()))
    half = len(pieces) // 2
    came = [flipped(group, order[0]) for group in pieces[half:]]
    groups = [
        [add(*pair) for pair in zip(cut(kept), cut(got))] for kept, got in zip(pieces[:half], came)
    ]
    for bit in order[1:]:
        groups, late = lax.optimization_barrier((groups, late))
        half = len(groups) // 2
        groups = [
            [add(kept, flipped(sent, bit)) for kept, sent in zip(*pair)]
            for pair in zip(groups[:half], groups[half:])
        ]
    total = 0.0
    for k, part in enumerate(groups[0]):
        if hop:
            part = moved(part, ("section", "expert"), lambda s, e, k=k: (s + hop, (e - k) % count))
        elif k:
            part = moved(part, ("expert",), lambda e, k=k: ((e - k) % count,))
        total = total + part.astype(F32)
    return total, late


def summed(block):
    for bit in reversed(flips()):
        block = block + flipped(block, bit)
    count = lax.axis_size("expert")
    total = block
    for k in range(1, count):
        total = total + moved(block, ("expert",), lambda e, k=k: ((e + k) % count,))
    return total


def across(block, distance):
    return moved(block, ("section",), lambda s: (s + distance,))


def swapped(block):
    return moved(block, ("section",), lambda s: (lax.axis_size("section") - 1 - s,))


def input_grad(layer_in, upstream, d_hidden, gain_row):
    values = layer_in.astype(F32)
    inv_rms = lax.rsqrt(jnp.mean(values * values, axis=-1, keepdims=True) + EPSILON)
    weighted = gain_row * d_hidden
    mean = jnp.mean(values * weighted, axis=-1, keepdims=True)
    cubed = inv_rms * inv_rms * inv_rms
    d_in = upstream.astype(F32) + inv_rms * weighted - values * cubed * mean
    return d_in.astype(BF16)


def per_device(inputs, cotangent, norm_gain, router, w_gate, w_up, w_down, routes):
    section = lax.axis_index("section")
    at_start = section == 0
    micro, toks, width = inputs.shape
    experts, top_k = router.shape[2], routes.shape[3]
    capacity = 3 * top_k * toks // (2 * experts)
    peers = lax.axis_size("expert") * lax.axis_size("dp")
    own = micro * toks
    tokens, rows = peers * own, peers * micro * capacity
    weights = (w_gate[0, 0], w_up[0, 0], w_down[0, 0])
    hidden_units = weights[0].shape[1]
    gain_row = norm_gain[0].astype(F32)
    blank = jnp.zeros((LANES - 1 - experts, width), BF16)
    router_w = jnp.concatenate([router[0].T, blank, norm_gain], axis=0)
    kept = -(-experts // 8) * 8
    shape = jax.ShapeDtypeStruct
    dot_flops = 2 * rows * width * hidden_units
    row_block, lane_block = pltpu.VMEM((rows, width), BF16), pltpu.VMEM((rows, LANES), F32)
    d_block = pltpu.VMEM((rows, hidden_units), BF16)

    mine = jnp.where(at_start, inputs, cotangent).reshape(own, width)
    tail = jnp.pad(routes[0].reshape(own, top_k).astype(BF16), ((0, 0), (0, LANES - top_k)))
    payload = jnp.concatenate([mine, tail], axis=1)
    with_gain = jnp.concatenate([mine, jnp.pad(norm_gain, ((0, 7), (0, 0)))], axis=0)
    pieces, swap = lax.optimization_barrier((gathered(payload), swapped(with_gain)))
    theirs, their_gain = swap[:own], swap[own].astype(F32)
    out, place, pick, hidden, info, stash_a, stash_b = expert_call(
        first_kernel, pieces, [router_w], weights,
        [shape((tokens, rows), BF16), shape((rows, tokens), BF16),
         shape((rows, width), BF16), shape((2, rows, LANES), F32),
         shape((rows, hidden_units), BF16), shape((rows, hidden_units), BF16)],
        [row_block, d_block],
        3 * dot_flops,
    )
    acts_mid = (theirs.astype(F32) + combined(out, 1)[0]).astype(BF16)

    pieces, acts_start = lax.optimization_barrier((gathered(acts_mid), across(acts_mid, -1)))
    back, active, prob, rg, gate_t, up_t = expert_call(
        middle_kernel, pieces,
        [router_w, place, pick, info, stash_a], weights,
        [shape((rows, hidden_units), BF16), shape((rows, LANES), F32), shape((kept, width), F32)],
        [row_block, row_block, d_block, d_block, lane_block,
         pltpu.SemaphoreType.DMA((hidden_units // tile_of(hidden_units, 512),))],
        4 * dot_flops, far=[shape((hidden_units, width), BF16)] * 2,
    )
    grads_mid = input_grad(acts_start, theirs, combined(back, -1)[0], their_gain)

    out, rg = expert_call(
        last_kernel, gathered(grads_mid),
        [router_w, place, pick, info, hidden, prob, rg, stash_a, stash_b, active],
        (gate_t, up_t, weights[2]),
        [shape((kept, width), F32)],
        [row_block, d_block, d_block, lane_block],
        3 * dot_flops, by_rows=True,
    )
    grads_end = across(grads_mid, 1)
    total, rg = combined(out, late=rg)
    router_total = summed(rg)[:experts].T
    grads_start = input_grad(mine, grads_mid, total, gain_row)
    acts_end = (acts_mid.astype(F32) + total).astype(BF16)
    acts = jnp.where(at_start, acts_start, acts_end).reshape(1, micro, toks, width)
    grads = jnp.where(at_start, grads_start, grads_end).reshape(1, micro, toks, width)
    return acts, grads, router_total[None]


def solution(mesh):
    placed = (
        P(None, GROUP, None),
        P(None, GROUP, None),
        P("section", None),
        P("section", None, None),
        P("section", "expert", None, "dp"),
        P("section", "expert", None, "dp"),
        P("section", "expert", "dp", None),
        P("section", None, GROUP, None),
    )
    return jax.shard_map(
        per_device,
        mesh=mesh,
        in_specs=placed,
        out_specs=(
            P("section", None, GROUP, None),
            P("section", None, GROUP, None),
            P("section", None, None),
        ),
        check_vma=False,
    )
```

profile of v0, /device:TPU:0, one launch (start us, length us, event | category | flops | bytes accessed | tf_op | source)
XLA Modules:
  0.0 192.3 jit_solution(16249187122123761860)
XLA Ops:
  2.4 5.1 %collective-permute-start.2 = (bf16[16,3200]{1,0:T(8,128)(2,1)S(1)}, bf16[16,3200]{1,0:T(8,128)(2,1)S(1)}, u32[]{:S(2)}, u32[]{:S(2)}) collective-permute-start(bf16[16,3200]{1,0:T(8,128)(2,1)S(1)} %fusion.13.refs_0_), channel_id=1, source_target_pairs={{0,12},{4,0},{8,4},{12,8},{1,13},{5,1},{9,5},{13,9},{2,14},{6,2},{... | collective-permute-start | bytes 307208 | tf_op jit(solution)/shard_map/ppermute | solution.py:404
  8.2 1.6 collective-permute-start.15
  9.8 1.0 collective-permute-start.1
  10.8 1.5 collective-permute-start.3
  12.8 4.0 %collective-permute-done.refs_1_ = bf16[16,3200]{1,0:T(8,128)(2,1)S(1)} collective-permute-done((bf16[16,3200]{1,0:T(8,128)(2,1)S(1)}, bf16[16,3200]{1,0:T(8,128)(2,1)S(1)}, u32[]{:S(2)}, u32[]{:S(2)}) %collective-permute-start) | collective-permute-done | bytes 102432 | tf_op jit(solution)/shard_map/ppermute | solution.py:404
  16.8 1.5 collective-permute-start.4
  19.1 1.5 collective-permute-start.5
  21.3 1.0 collective-permute-done.4.refs_5_
  22.3 1.5 collective-permute-done.5.refs_6_
  25.8 16.9 %shard_map.103 = (bf16[64,3072]{1,0:T(8,128)(2,1)S(1)}, bf16[64,3072]{1,0:T(8,128)(2,1)S(1)}, bf16[64,3072]{1,0:T(8,128)(2,1)S(1)}, bf16[64,3072]{1,0:T(8,128)(2...) custom-call(bf16[16,3200]{1,0:T(8,128)(2,1)S(1)} %fusion.13.refs_0_,, ...), custom_call_target="tpu_custom_call" | custom-call | flops 7247757312 | bytes 37748736 | tf_op jit(solution)/shard_map/pallas_call | solution.py:383
  43.3 1.2 collective-permute-done.17
  45.2 1.5 collective-permute-start.18
  47.3 1.5 collective-permute-start.22
  49.3 1.6 collective-permute-done.18
  50.9 1.3 collective-permute-start.19
  53.0 1.3 collective-permute-start.21
  55.1 1.3 collective-permute-start.23
  56.5 1.3 collective-permute-start.25
  57.9 1.6 collective-permute-done.23
  59.4 1.2 collective-permute-done.25
  60.7 1.5 collective-permute-start.28
  62.3 2.5 %collective-permute-start.26 = (bf16[16,3072]{1,0:T(8,128)(2,1)S(1)}, bf16[16,3072]{1,0:T(8,128)(2,1)S(1)}, u32[]{:S(2)}, u32[]{:S(2)}) collective-permute-start(bf16[16,3072]{1,0:T(8,128)(2,1)S(1)} %fusion.2.refs_0_), channel_id=1, source_target_pairs={{0,4},{4,8},{8,12},{12,0},{1,5},{5,9},{9,13},{13,1},{2,6},{6,10},{... | collective-permute-start | bytes 294920 | tf_op jit(solution)/shard_map/ppermute | solution.py:404
  64.8 1.4 collective-permute-start.27
  66.5 3.0 %collective-permute-done.28.refs_3_ = bf16[16,3072]{1,0:T(8,128)(2,1)S(1)} collective-permute-done((bf16[16,3072]{1,0:T(8,128)(2,1)S(1)}, bf16[16,3072]{1,0:T(8,128)(2,1)S(1)}, u32[]{:S(2)}, u32[]{:S(2)}) %collective-permute-start.28) | collective-permute-done | bytes 98336 | tf_op jit(solution)/shard_map/ppermute | solution.py:404
  69.5 1.3 collective-permute-start.41
  70.8 2.1 %collective-permute-start.30 = (bf16[16,3072]{1,0:T(8,128)(2,1)S(1)}, bf16[16,3072]{1,0:T(8,128)(2,1)S(1)}, u32[]{:S(2)}, u32[]{:S(2)}) collective-permute-start(bf16[16,3072]{1,0:T(8,128)(2,1)S(1)} %collective-permute-done.26.refs_1_), channel_id=1, source_target_pairs={{0,2},{1,3},{2,0},{3,1},{4,6},{5,7},{6,4},{7,5},{8,10},{9,11},{10,... | collective-permute-start | bytes 294920 | tf_op jit(solution)/shard_map/ppermute | solution.py:404
  73.5 1.2 collective-permute-start.31
  76.6 1.4 collective-permute-done.31.refs_6_
  80.0 16.5 %shard_map.104 = (bf16[64,3072]{1,0:T(8,128)(2,1)S(1)}, bf16[64,3072]{1,0:T(8,128)(2,1)S(1)}, bf16[64,3072]{1,0:T(8,128)(2,1)S(1)}, bf16[64,3072]{1,0:T(8,128)(2...) custom-call(bf16[16,3072]{1,0:T(8,128)(2,1)S(1)} %fusion.2.refs_0_, ...), custom_call_target="tpu_custom_call" | custom-call | flops 9663676416 | bytes 37748736 | tf_op jit(solution)/shard_map/pallas_call | solution.py:383
  97.1 1.2 collective-permute-done.43
  99.0 1.3 collective-permute-start.44
  101.1 1.2 collective-permute-start.48
  103.1 1.6 collective-permute-done.44
  104.7 1.3 collective-permute-start.45
  106.8 1.3 collective-permute-start.47
  108.9 1.3 collective-permute-start.49
  110.5 1.3 collective-permute-start.51
  111.8 5.6 %collective-permute-done.45 = bf16[16,3072]{1,0:T(8,128)(2,1)S(1)} collective-permute-done((bf16[16,3072]{1,0:T(8,128)(2,1)S(1)}, bf16[16,3072]{1,0:T(8,128)(2,1)S(1)}, u32[]{:S(2)}, u32[]{:S(2)}) %collective-permute-start.45) | collective-permute-done | bytes 98336 | tf_op jit(solution)/shard_map/ppermute | solution.py:404
  117.4 5.0 %collective-permute-done.47 = bf16[16,3072]{1,0:T(8,128)(2,1)S(1)} collective-permute-done((bf16[16,3072]{1,0:T(8,128)(2,1)S(1)}, bf16[16,3072]{1,0:T(8,128)(2,1)S(1)}, u32[]{:S(2)}, u32[]{:S(2)}) %collective-permute-start.47) | collective-permute-done | bytes 98336 | tf_op jit(solution)/shard_map/ppermute | solution.py:404
  122.3 5.2 %collective-permute-done.49 = bf16[16,3072]{1,0:T(8,128)(2,1)S(1)} collective-permute-done((bf16[16,3072]{1,0:T(8,128)(2,1)S(1)}, bf16[16,3072]{1,0:T(8,128)(2,1)S(1)}, u32[]{:S(2)}, u32[]{:S(2)}) %collective-permute-start.49) | collective-permute-done | bytes 98336 | tf_op jit(solution)/shard_map/ppermute | solution.py:404
  128.7 1.3 collective-permute-start.52
  130.0 1.6 collective-permute-start.53
  131.7 1.3 collective-permute-start.55
  133.0 1.7 collective-permute-done.54.refs_3_
  134.8 1.7 collective-permute-done.52.refs_1_
  137.0 1.6 collective-permute-done.53.refs_2_
  138.6 1.3 collective-permute-start.57
  140.4 1.4 collective-permute-done.56.refs_5_
  141.8 1.4 collective-permute-done.57.refs_6_
  145.2 18.8 %shard_map.105 = (bf16[64,3072]{1,0:T(8,128)(2,1)S(1)}, bf16[64,3072]{1,0:T(8,128)(2,1)S(1)}, bf16[64,3072]{1,0:T(8,128)(2,1)S(1)}, bf16[64,3072]{1,0:T(8,128)(2,1)S(1)}, f32[8,3072]{1,0:T(8,128)S(1)}) custom-call(bf16[16,3072]{1,0:T(8,128)(2,1)S(1)} %fusion.4.refs_0_, bf16[16,3072]{1,0:T(8,128)(2,1)S(1)} %collective-permute-done.52.refs_1_, ...), custom_call_target="tpu_custom_call" | custom-call | flops 7247757312 | bytes 37748736 | tf_op jit(solution)/shard_map/pallas_call | solution.py:383
  164.7 1.1 collective-permute-done.68
  166.8 1.3 collective-permute-start.70
  168.9 1.3 collective-permute-start.74
  171.0 1.3 collective-permute-start.78
  172.5 2.1 %collective-permute-start.71 = (bf16[16,3072]{1,0:T(8,128)(2,1)S(1)}, bf16[16,3072]{1,0:T(8,128)(2,1)S(1)}, u32[]{:S(2)}, u32[]{:S(2)}) collective-permute-start(bf16[16,3072]{1,0:T(8,128)(2,1)S(1)} %add_convert_fusion.3), channel_id=1, source_target_pairs={{0,12},{4,0},{8,4},{12,8},{1,13},{5,1},{9,5},{13,9},{2,14},{6,2},{... | collective-permute-start | bytes 294920 | tf_op jit(solution)/shard_map/ppermute | solution.py:404
  174.6 1.0 collective-permute-start.73
  176.7 1.5 collective-permute-start.75
  178.3 1.8 collective-permute-done.78
  180.1 1.3 collective-permute-start.76
  181.4 1.5 collective-permute-start.79
  182.9 1.2 collective-permute-start.80
  184.1 1.3 collective-permute-start.81
  186.4 2.7 %collective-permute-done.79 = f32[8,3072]{1,0:T(8,128)S(1)} collective-permute-done((f32[8,3072]{1,0:T(8,128)S(1)}, f32[8,3072]{1,0:T(8,128)S(1)}, u32[]{:S(2)}, u32[]{:S(2)}) %collective-permute-start.79) | collective-permute-done | bytes 98336 | tf_op jit(solution)/shard_map/ppermute | solution.py:404
  189.1 2.5 %collective-permute-done.80 = f32[8,3072]{1,0:T(8,128)S(1)} collective-permute-done((f32[8,3072]{1,0:T(8,128)S(1)}, f32[8,3072]{1,0:T(8,128)S(1)}, u32[]{:S(2)}, u32[]{:S(2)}) %collective-permute-start.80) | collective-permute-done | bytes 98336 | tf_op jit(solution)/shard_map/ppermute | solution.py:404
  (152 shorter events, 30.8 us)
Async XLA Ops:
  2.4 9.9 %collective-permute-start.2 = (bf16[16,3200]{1,0:T(8,128)(2,1)S(1)}, bf16[16,3200]{1,0:T(8,128)(2,1)S(1)}, u32[]{:S(2)}, u32[]{:S(2)}) collective-permute-start(bf16[16,3200]{1,0:T(8,128)(2,1)S(1)} %fusion.13.refs_0_), channel_id=1, source_target_pairs={{0,12},{4,0},{8,4},{12,8},{1,13},{5,1},{9,5},{13,9},{2,14},{6,2},{... | collective-permute-start | bytes 307208 | tf_op jit(solution)/shard_map/ppermute | solution.py:404
  8.2 13.0 %collective-permute-start.15 = (bf16[24,3072]{1,0:T(8,128)(2,1)S(1)}, bf16[24,3072]{1,0:T(8,128)(2,1)S(1)}, u32[]{:S(2)}, u32[]{:S(2)}) collective-permute-start(bf16[24,3072]{1,0:T(8,128)(2,1)S(1)} %fusion.12), channel_id=1, source_target_pairs={{0,16},{16,0},{1,17},{17,1},{2,18},{18,2},{3,19},{19,3},{4,20},{20... | collective-permute-start | bytes 442376 | tf_op jit(solution)/shard_map/ppermute | solution.py:404
  9.8 7.1 %collective-permute-start = (bf16[16,3200]{1,0:T(8,128)(2,1)S(1)}, bf16[16,3200]{1,0:T(8,128)(2,1)S(1)}, u32[]{:S(2)}, u32[]{:S(2)}) collective-permute-start(bf16[16,3200]{1,0:T(8,128)(2,1)S(1)} %fusion.13.refs_0_), channel_id=1, source_target_pairs={{0,4},{4,8},{8,12},{12,0},{1,5},{5,9},{9,13},{13,1},{2,6},{6,10},{... | collective-permute-start | bytes 307208 | tf_op jit(solution)/shard_map/ppermute | solution.py:404
  9.8 9.4 %collective-permute-start.1 = (bf16[16,3200]{1,0:T(8,128)(2,1)S(1)}, bf16[16,3200]{1,0:T(8,128)(2,1)S(1)}, u32[]{:S(2)}, u32[]{:S(2)}) collective-permute-start(bf16[16,3200]{1,0:T(8,128)(2,1)S(1)} %fusion.13.refs_0_), channel_id=1, source_target_pairs={{0,8},{4,12},{8,0},{12,4},{1,9},{5,13},{9,1},{13,5},{2,10},{6,14},... | collective-permute-start | bytes 307208 | tf_op jit(solution)/shard_map/ppermute | solution.py:404
  10.8 9.8 %collective-permute-start.3 = (bf16[16,3200]{1,0:T(8,128)(2,1)S(1)}, bf16[16,3200]{1,0:T(8,128)(2,1)S(1)}, u32[]{:S(2)}, u32[]{:S(2)}) collective-permute-start(bf16[16,3200]{1,0:T(8,128)(2,1)S(1)} %fusion.13.refs_0_), channel_id=1, source_target_pairs={{0,2},{1,3},{2,0},{3,1},{4,6},{5,7},{6,4},{7,5},{8,10},{9,11},{10,... | collective-permute-start | bytes 307208 | tf_op jit(solution)/shard_map/ppermute | solution.py:404
  12.3 8.3 %collective-permute-start.6 = (bf16[16,3200]{1,0:T(8,128)(2,1)S(1)}, bf16[16,3200]{1,0:T(8,128)(2,1)S(1)}, u32[]{:S(2)}, u32[]{:S(2)}) collective-permute-start(bf16[16,3200]{1,0:T(8,128)(2,1)S(1)} %collective-permute-done.2.refs_3_), channel_id=1, source_target_pairs={{0,2},{1,3},{2,0},{3,1},{4,6},{5,7},{6,4},{7,5},{8,10},{9,11},{10,... | collective-permute-start | bytes 307208 | tf_op jit(solution)/shard_map/ppermute | solution.py:404
  16.8 5.5 %collective-permute-start.4 = (bf16[16,3200]{1,0:T(8,128)(2,1)S(1)}, bf16[16,3200]{1,0:T(8,128)(2,1)S(1)}, u32[]{:S(2)}, u32[]{:S(2)}) collective-permute-start(bf16[16,3200]{1,0:T(8,128)(2,1)S(1)} %collective-permute-done.refs_1_), channel_id=1, source_target_pairs={{0,2},{1,3},{2,0},{3,1},{4,6},{5,7},{6,4},{7,5},{8,10},{9,11},{10,... | collective-permute-start | bytes 307208 | tf_op jit(solution)/shard_map/ppermute | solution.py:404
  19.1 4.7 %collective-permute-start.5 = (bf16[16,3200]{1,0:T(8,128)(2,1)S(1)}, bf16[16,3200]{1,0:T(8,128)(2,1)S(1)}, u32[]{:S(2)}, u32[]{:S(2)}) collective-permute-start(bf16[16,3200]{1,0:T(8,128)(2,1)S(1)} %collective-permute-done.1.refs_2_), channel_id=1, source_target_pairs={{0,2},{1,3},{2,0},{3,1},{4,6},{5,7},{6,4},{7,5},{8,10},{9,11},{10,... | collective-permute-start | bytes 307208 | tf_op jit(solution)/shard_map/ppermute | solution.py:404
  20.6 3.2 %collective-permute-start.11 = (bf16[16,3200]{1,0:T(8,128)(2,1)S(1)}, bf16[16,3200]{1,0:T(8,128)(2,1)S(1)}, u32[]{:S(2)}, u32[]{:S(2)}) collective-permute-start(bf16[16,3200]{1,0:T(8,128)(2,1)S(1)} %collective-permute-done.3.refs_4_), channel_id=1, source_target_pairs={{0,1},{1,0},{2,3},{3,2},{4,5},{5,4},{6,7},{7,6},{8,9},{9,8},{10,11... | collective-permute-start | bytes 307208 | tf_op jit(solution)/shard_map/ppermute | solution.py:404
  20.6 3.7 %collective-permute-start.10 = (bf16[16,3200]{1,0:T(8,128)(2,1)S(1)}, bf16[16,3200]{1,0:T(8,128)(2,1)S(1)}, u32[]{:S(2)}, u32[]{:S(2)}) collective-permute-start(bf16[16,3200]{1,0:T(8,128)(2,1)S(1)} %collective-permute-done.2.refs_3_), channel_id=1, source_target_pairs={{0,1},{1,0},{2,3},{3,2},{4,5},{5,4},{6,7},{7,6},{8,9},{9,8},{10,11... | collective-permute-start | bytes 307208 | tf_op jit(solution)/shard_map/ppermute | solution.py:404
  21.1 3.2 %collective-permute-start.7 = (bf16[16,3200]{1,0:T(8,128)(2,1)S(1)}, bf16[16,3200]{1,0:T(8,128)(2,1)S(1)}, u32[]{:S(2)}, u32[]{:S(2)}) collective-permute-start(bf16[16,3200]{1,0:T(8,128)(2,1)S(1)} %fusion.13.refs_0_), channel_id=1, source_target_pairs={{0,1},{1,0},{2,3},{3,2},{4,5},{5,4},{6,7},{7,6},{8,9},{9,8},{10,11... | collective-permute-start | bytes 307208 | tf_op jit(solution)/shard_map/ppermute | solution.py:404
  22.3 3.4 %collective-permute-start.8 = (bf16[16,3200]{1,0:T(8,128)(2,1)S(1)}, bf16[16,3200]{1,0:T(8,128)(2,1)S(1)}, u32[]{:S(2)}, u32[]{:S(2)}) collective-permute-start(bf16[16,3200]{1,0:T(8,128)(2,1)S(1)} %collective-permute-done.refs_1_), channel_id=1, source_target_pairs={{0,1},{1,0},{2,3},{3,2},{4,5},{5,4},{6,7},{7,6},{8,9},{9,8},{10,11... | collective-permute-start | bytes 307208 | tf_op jit(solution)/shard_map/ppermute | solution.py:404
  45.2 5.7 %collective-permute-start.18 = (bf16[16,3072]{1,0:T(8,128)(2,1)S(1)}, bf16[16,3072]{1,0:T(8,128)(2,1)S(1)}, u32[]{:S(2)}, u32[]{:S(2)}) collective-permute-start(bf16[16,3072]{1,0:T(8,128)(2,1)S(1)} %get-tuple-element.124), channel_id=1, source_target_pairs={{0,2},{1,3},{2,0},{3,1},{4,6},{5,7},{6,4},{7,5},{8,10},{9,11},{10,... | collective-permute-start | bytes 294920 | tf_op jit(solution)/shard_map/ppermute | solution.py:404
  46.7 6.2 %collective-permute-start.20 = (bf16[16,3072]{1,0:T(8,128)(2,1)S(1)}, bf16[16,3072]{1,0:T(8,128)(2,1)S(1)}, u32[]{:S(2)}, u32[]{:S(2)}) collective-permute-start(bf16[16,3072]{1,0:T(8,128)(2,1)S(1)} %get-tuple-element.126), channel_id=1, source_target_pairs={{0,2},{1,3},{2,0},{3,1},{4,6},{5,7},{6,4},{7,5},{8,10},{9,11},{10,... | collective-permute-start | bytes 294920 | tf_op jit(solution)/shard_map/ppermute | solution.py:404
  47.3 7.8 %collective-permute-start.22 = (bf16[16,3072]{1,0:T(8,128)(2,1)S(1)}, bf16[16,3072]{1,0:T(8,128)(2,1)S(1)}, u32[]{:S(2)}, u32[]{:S(2)}) collective-permute-start(bf16[16,3072]{1,0:T(8,128)(2,1)S(1)} %get-tuple-element.128), channel_id=1, source_target_pairs={{0,2},{1,3},{2,0},{3,1},{4,6},{5,7},{6,4},{7,5},{8,10},{9,11},{10,... | collective-permute-start | bytes 294920 | tf_op jit(solution)/shard_map/ppermute | solution.py:404
  48.7 7.8 %collective-permute-start.24 = (bf16[16,3072]{1,0:T(8,128)(2,1)S(1)}, bf16[16,3072]{1,0:T(8,128)(2,1)S(1)}, u32[]{:S(2)}, u32[]{:S(2)}) collective-permute-start(bf16[16,3072]{1,0:T(8,128)(2,1)S(1)} %get-tuple-element.130), channel_id=1, source_target_pairs={{0,2},{1,3},{2,0},{3,1},{4,6},{5,7},{6,4},{7,5},{8,10},{9,11},{10,... | collective-permute-start | bytes 294920 | tf_op jit(solution)/shard_map/ppermute | solution.py:404
  50.9 7.0 %collective-permute-start.19 = (bf16[16,3072]{1,0:T(8,128)(2,1)S(1)}, bf16[16,3072]{1,0:T(8,128)(2,1)S(1)}, u32[]{:S(2)}, u32[]{:S(2)}) collective-permute-start(bf16[16,3072]{1,0:T(8,128)(2,1)S(1)} %add_convert_fusion.28), channel_id=1, source_target_pairs={{0,16},{4,20},{8,24},{12,28},{1,17},{5,21},{9,25},{13,29},{2,18},{... | collective-permute-start | bytes 294920 | tf_op jit(solution)/shard_map/ppermute | solution.py:404
  53.0 4.9 %collective-permute-start.21 = (bf16[16,3072]{1,0:T(8,128)(2,1)S(1)}, bf16[16,3072]{1,0:T(8,128)(2,1)S(1)}, u32[]{:S(2)}, u32[]{:S(2)}) collective-permute-start(bf16[16,3072]{1,0:T(8,128)(2,1)S(1)} %add_convert_fusion.27), channel_id=1, source_target_pairs={{0,28},{4,16},{8,20},{12,24},{1,29},{5,17},{9,21},{13,25},{2,30},{... | collective-permute-start | bytes 294920 | tf_op jit(solution)/shard_map/ppermute | solution.py:404
  55.1 4.3 %collective-permute-start.23 = (bf16[16,3072]{1,0:T(8,128)(2,1)S(1)}, bf16[16,3072]{1,0:T(8,128)(2,1)S(1)}, u32[]{:S(2)}, u32[]{:S(2)}) collective-permute-start(bf16[16,3072]{1,0:T(8,128)(2,1)S(1)} %add_convert_fusion.26), channel_id=1, source_target_pairs={{0,24},{4,28},{8,16},{12,20},{1,25},{5,29},{9,17},{13,21},{2,26},{... | collective-permute-start | bytes 294920 | tf_op jit(solution)/shard_map/ppermute | solution.py:404
  56.5 4.1 %collective-permute-start.25 = (bf16[16,3072]{1,0:T(8,128)(2,1)S(1)}, bf16[16,3072]{1,0:T(8,128)(2,1)S(1)}, u32[]{:S(2)}, u32[]{:S(2)}) collective-permute-start(bf16[16,3072]{1,0:T(8,128)(2,1)S(1)} %add_convert_fusion.25), channel_id=1, source_target_pairs={{0,20},{4,24},{8,28},{12,16},{1,21},{5,25},{9,29},{13,17},{2,22},{... | collective-permute-start | bytes 294920 | tf_op jit(solution)/shard_map/ppermute | solution.py:404
  60.7 8.8 %collective-permute-start.28 = (bf16[16,3072]{1,0:T(8,128)(2,1)S(1)}, bf16[16,3072]{1,0:T(8,128)(2,1)S(1)}, u32[]{:S(2)}, u32[]{:S(2)}) collective-permute-start(bf16[16,3072]{1,0:T(8,128)(2,1)S(1)} %fusion.2.refs_0_), channel_id=1, source_target_pairs={{0,12},{4,0},{8,4},{12,8},{1,13},{5,1},{9,5},{13,9},{2,14},{6,2},{... | collective-permute-start | bytes 294920 | tf_op jit(solution)/shard_map/ppermute | solution.py:404
  62.3 8.6 %collective-permute-start.26 = (bf16[16,3072]{1,0:T(8,128)(2,1)S(1)}, bf16[16,3072]{1,0:T(8,128)(2,1)S(1)}, u32[]{:S(2)}, u32[]{:S(2)}) collective-permute-start(bf16[16,3072]{1,0:T(8,128)(2,1)S(1)} %fusion.2.refs_0_), channel_id=1, source_target_pairs={{0,4},{4,8},{8,12},{12,0},{1,5},{5,9},{9,13},{13,1},{2,6},{6,10},{... | collective-permute-start | bytes 294920 | tf_op jit(solution)/shard_map/ppermute | solution.py:404
  64.8 8.6 %collective-permute-start.27 = (bf16[16,3072]{1,0:T(8,128)(2,1)S(1)}, bf16[16,3072]{1,0:T(8,128)(2,1)S(1)}, u32[]{:S(2)}, u32[]{:S(2)}) collective-permute-start(bf16[16,3072]{1,0:T(8,128)(2,1)S(1)} %fusion.2.refs_0_), channel_id=1, source_target_pairs={{0,8},{4,12},{8,0},{12,4},{1,9},{5,13},{9,1},{13,5},{2,10},{6,14},... | collective-permute-start | bytes 294920 | tf_op jit(solution)/shard_map/ppermute | solution.py:404
  66.2 8.5 %collective-permute-start.29 = (bf16[16,3072]{1,0:T(8,128)(2,1)S(1)}, bf16[16,3072]{1,0:T(8,128)(2,1)S(1)}, u32[]{:S(2)}, u32[]{:S(2)}) collective-permute-start(bf16[16,3072]{1,0:T(8,128)(2,1)S(1)} %fusion.2.refs_0_), channel_id=1, source_target_pairs={{0,2},{1,3},{2,0},{3,1},{4,6},{5,7},{6,4},{7,5},{8,10},{9,11},{10,... | collective-permute-start | bytes 294920 | tf_op jit(solution)/shard_map/ppermute | solution.py:404
  69.5 5.1 %collective-permute-start.32 = (bf16[16,3072]{1,0:T(8,128)(2,1)S(1)}, bf16[16,3072]{1,0:T(8,128)(2,1)S(1)}, u32[]{:S(2)}, u32[]{:S(2)}) collective-permute-start(bf16[16,3072]{1,0:T(8,128)(2,1)S(1)} %collective-permute-done.28.refs_3_), channel_id=1, source_target_pairs={{0,2},{1,3},{2,0},{3,1},{4,6},{5,7},{6,4},{7,5},{8,10},{9,11},{10,... | collective-permute-start | bytes 294920 | tf_op jit(solution)/shard_map/ppermute | solution.py:404
  69.5 6.6 %collective-permute-start.41 = (bf16[16,3072]{1,0:T(8,128)(2,1)S(1)}, bf16[16,3072]{1,0:T(8,128)(2,1)S(1)}, u32[]{:S(2)}, u32[]{:S(2)}) collective-permute-start(bf16[16,3072]{1,0:T(8,128)(2,1)S(1)} %fusion.2.refs_0_), channel_id=1, source_target_pairs={{16,0},{17,1},{18,2},{19,3},{20,4},{21,5},{22,6},{23,7},{24,8},{25... | collective-permute-start | bytes 294920 | tf_op jit(solution)/shard_map/ppermute | solution.py:404
  70.8 5.5 %collective-permute-start.30 = (bf16[16,3072]{1,0:T(8,128)(2,1)S(1)}, bf16[16,3072]{1,0:T(8,128)(2,1)S(1)}, u32[]{:S(2)}, u32[]{:S(2)}) collective-permute-start(bf16[16,3072]{1,0:T(8,128)(2,1)S(1)} %collective-permute-done.26.refs_1_), channel_id=1, source_target_pairs={{0,2},{1,3},{2,0},{3,1},{4,6},{5,7},{6,4},{7,5},{8,10},{9,11},{10,... | collective-permute-start | bytes 294920 | tf_op jit(solution)/shard_map/ppermute | solution.py:404
  73.5 4.6 %collective-permute-start.31 = (bf16[16,3072]{1,0:T(8,128)(2,1)S(1)}, bf16[16,3072]{1,0:T(8,128)(2,1)S(1)}, u32[]{:S(2)}, u32[]{:S(2)}) collective-permute-start(bf16[16,3072]{1,0:T(8,128)(2,1)S(1)} %collective-permute-done.27.refs_2_), channel_id=1, source_target_pairs={{0,2},{1,3},{2,0},{3,1},{4,6},{5,7},{6,4},{7,5},{8,10},{9,11},{10,... | collective-permute-start | bytes 294920 | tf_op jit(solution)/shard_map/ppermute | solution.py:404
  74.7 3.4 %collective-permute-start.37 = (bf16[16,3072]{1,0:T(8,128)(2,1)S(1)}, bf16[16,3072]{1,0:T(8,128)(2,1)S(1)}, u32[]{:S(2)}, u32[]{:S(2)}) collective-permute-start(bf16[16,3072]{1,0:T(8,128)(2,1)S(1)} %collective-permute-done.29.refs_4_), channel_id=1, source_target_pairs={{0,1},{1,0},{2,3},{3,2},{4,5},{5,4},{6,7},{7,6},{8,9},{9,8},{10,11... | collective-permute-start | bytes 294920 | tf_op jit(solution)/shard_map/ppermute | solution.py:404
  74.7 3.9 %collective-permute-start.33 = (bf16[16,3072]{1,0:T(8,128)(2,1)S(1)}, bf16[16,3072]{1,0:T(8,128)(2,1)S(1)}, u32[]{:S(2)}, u32[]{:S(2)}) collective-permute-start(bf16[16,3072]{1,0:T(8,128)(2,1)S(1)} %fusion.2.refs_0_), channel_id=1, source_target_pairs={{0,1},{1,0},{2,3},{3,2},{4,5},{5,4},{6,7},{7,6},{8,9},{9,8},{10,11... | collective-permute-start | bytes 294920 | tf_op jit(solution)/shard_map/ppermute | solution.py:404
  76.1 2.5 %collective-permute-start.34 = (bf16[16,3072]{1,0:T(8,128)(2,1)S(1)}, bf16[16,3072]{1,0:T(8,128)(2,1)S(1)}, u32[]{:S(2)}, u32[]{:S(2)}) collective-permute-start(bf16[16,3072]{1,0:T(8,128)(2,1)S(1)} %collective-permute-done.26.refs_1_), channel_id=1, source_target_pairs={{0,1},{1,0},{2,3},{3,2},{4,5},{5,4},{6,7},{7,6},{8,9},{9,8},{10,11... | collective-permute-start | bytes 294920 | tf_op jit(solution)/shard_map/ppermute | solution.py:404
  76.4 2.7 %collective-permute-start.35 = (bf16[16,3072]{1,0:T(8,128)(2,1)S(1)}, bf16[16,3072]{1,0:T(8,128)(2,1)S(1)}, u32[]{:S(2)}, u32[]{:S(2)}) collective-permute-start(bf16[16,3072]{1,0:T(8,128)(2,1)S(1)} %collective-permute-done.27.refs_2_), channel_id=1, source_target_pairs={{0,1},{1,0},{2,3},{3,2},{4,5},{5,4},{6,7},{7,6},{8,9},{9,8},{10,11... | collective-permute-start | bytes 294920 | tf_op jit(solution)/shard_map/ppermute | solution.py:404
  99.0 5.7 %collective-permute-start.44 = (bf16[16,3072]{1,0:T(8,128)(2,1)S(1)}, bf16[16,3072]{1,0:T(8,128)(2,1)S(1)}, u32[]{:S(2)}, u32[]{:S(2)}) collective-permute-start(bf16[16,3072]{1,0:T(8,128)(2,1)S(1)} %get-tuple-element.161), channel_id=1, source_target_pairs={{0,2},{1,3},{2,0},{3,1},{4,6},{5,7},{6,4},{7,5},{8,10},{9,11},{10,... | collective-permute-start | bytes 294920 | tf_op jit(solution)/shard_map/ppermute | solution.py:404
  100.3 6.5 %collective-permute-start.46 = (bf16[16,3072]{1,0:T(8,128)(2,1)S(1)}, bf16[16,3072]{1,0:T(8,128)(2,1)S(1)}, u32[]{:S(2)}, u32[]{:S(2)}) collective-permute-start(bf16[16,3072]{1,0:T(8,128)(2,1)S(1)} %get-tuple-element.163), channel_id=1, source_target_pairs={{0,2},{1,3},{2,0},{3,1},{4,6},{5,7},{6,4},{7,5},{8,10},{9,11},{10,... | collective-permute-start | bytes 294920 | tf_op jit(solution)/shard_map/ppermute | solution.py:404
  101.1 7.8 %collective-permute-start.48 = (bf16[16,3072]{1,0:T(8,128)(2,1)S(1)}, bf16[16,3072]{1,0:T(8,128)(2,1)S(1)}, u32[]{:S(2)}, u32[]{:S(2)}) collective-permute-start(bf16[16,3072]{1,0:T(8,128)(2,1)S(1)} %get-tuple-element.165), channel_id=1, source_target_pairs={{0,2},{1,3},{2,0},{3,1},{4,6},{5,7},{6,4},{7,5},{8,10},{9,11},{10,... | collective-permute-start | bytes 294920 | tf_op jit(solution)/shard_map/ppermute | solution.py:404
  102.3 8.1 %collective-permute-start.50 = (bf16[16,3072]{1,0:T(8,128)(2,1)S(1)}, bf16[16,3072]{1,0:T(8,128)(2,1)S(1)}, u32[]{:S(2)}, u32[]{:S(2)}) collective-permute-start(bf16[16,3072]{1,0:T(8,128)(2,1)S(1)} %get-tuple-element.167), channel_id=1, source_target_pairs={{0,2},{1,3},{2,0},{3,1},{4,6},{5,7},{6,4},{7,5},{8,10},{9,11},{10,... | collective-permute-start | bytes 294920 | tf_op jit(solution)/shard_map/ppermute | solution.py:404
  104.7 12.7 %collective-permute-start.45 = (bf16[16,3072]{1,0:T(8,128)(2,1)S(1)}, bf16[16,3072]{1,0:T(8,128)(2,1)S(1)}, u32[]{:S(2)}, u32[]{:S(2)}) collective-permute-start(bf16[16,3072]{1,0:T(8,128)(2,1)S(1)} %add_convert_fusion.16), channel_id=1, source_target_pairs={{16,0},{20,4},{24,8},{28,12},{17,1},{21,5},{25,9},{29,13},{18,2},{... | collective-permute-start | bytes 294920 | tf_op jit(solution)/shard_map/ppermute | solution.py:404
  106.8 15.5 %collective-permute-start.47 = (bf16[16,3072]{1,0:T(8,128)(2,1)S(1)}, bf16[16,3072]{1,0:T(8,128)(2,1)S(1)}, u32[]{:S(2)}, u32[]{:S(2)}) collective-permute-start(bf16[16,3072]{1,0:T(8,128)(2,1)S(1)} %add_convert_fusion.15), channel_id=1, source_target_pairs={{16,12},{20,0},{24,4},{28,8},{17,13},{21,1},{25,5},{29,9},{18,14},... | collective-permute-start | bytes 294920 | tf_op jit(solution)/shard_map/ppermute | solution.py:404
  108.9 18.6 %collective-permute-start.49 = (bf16[16,3072]{1,0:T(8,128)(2,1)S(1)}, bf16[16,3072]{1,0:T(8,128)(2,1)S(1)}, u32[]{:S(2)}, u32[]{:S(2)}) collective-permute-start(bf16[16,3072]{1,0:T(8,128)(2,1)S(1)} %add_convert_fusion.14), channel_id=1, source_target_pairs={{16,8},{20,12},{24,0},{28,4},{17,9},{21,13},{25,1},{29,5},{18,10},... | collective-permute-start | bytes 294920 | tf_op jit(solution)/shard_map/ppermute | solution.py:404
  110.5 17.1 %collective-permute-start.51 = (bf16[16,3072]{1,0:T(8,128)(2,1)S(1)}, bf16[16,3072]{1,0:T(8,128)(2,1)S(1)}, u32[]{:S(2)}, u32[]{:S(2)}) collective-permute-start(bf16[16,3072]{1,0:T(8,128)(2,1)S(1)} %add_convert_fusion.13), channel_id=1, source_target_pairs={{16,4},{20,8},{24,12},{28,0},{17,5},{21,9},{25,13},{29,1},{18,6},{... | collective-permute-start | bytes 294920 | tf_op jit(solution)/shard_map/ppermute | solution.py:404
  127.9 6.7 %collective-permute-start.54 = (bf16[16,3072]{1,0:T(8,128)(2,1)S(1)}, bf16[16,3072]{1,0:T(8,128)(2,1)S(1)}, u32[]{:S(2)}, u32[]{:S(2)}) collective-permute-start(bf16[16,3072]{1,0:T(8,128)(2,1)S(1)} %fusion.4.refs_0_), channel_id=1, source_target_pairs={{0,12},{4,0},{8,4},{12,8},{1,13},{5,1},{9,5},{13,9},{2,14},{6,2},{... | collective-permute-start | bytes 294920 | tf_op jit(solution)/shard_map/ppermute | solution.py:404
  128.7 7.7 %collective-permute-start.52 = (bf16[16,3072]{1,0:T(8,128)(2,1)S(1)}, bf16[16,3072]{1,0:T(8,128)(2,1)S(1)}, u32[]{:S(2)}, u32[]{:S(2)}) collective-permute-start(bf16[16,3072]{1,0:T(8,128)(2,1)S(1)} %fusion.4.refs_0_), channel_id=1, source_target_pairs={{0,4},{4,8},{8,12},{12,0},{1,5},{5,9},{9,13},{13,1},{2,6},{6,10},{... | collective-permute-start | bytes 294920 | tf_op jit(solution)/shard_map/ppermute | solution.py:404
  130.0 8.6 %collective-permute-start.53 = (bf16[16,3072]{1,0:T(8,128)(2,1)S(1)}, bf16[16,3072]{1,0:T(8,128)(2,1)S(1)}, u32[]{:S(2)}, u32[]{:S(2)}) collective-permute-start(bf16[16,3072]{1,0:T(8,128)(2,1)S(1)} %fusion.4.refs_0_), channel_id=1, source_target_pairs={{0,8},{4,12},{8,0},{12,4},{1,9},{5,13},{9,1},{13,5},{2,10},{6,14},... | collective-permute-start | bytes 294920 | tf_op jit(solution)/shard_map/ppermute | solution.py:404
  131.7 8.2 %collective-permute-start.55 = (bf16[16,3072]{1,0:T(8,128)(2,1)S(1)}, bf16[16,3072]{1,0:T(8,128)(2,1)S(1)}, u32[]{:S(2)}, u32[]{:S(2)}) collective-permute-start(bf16[16,3072]{1,0:T(8,128)(2,1)S(1)} %fusion.4.refs_0_), channel_id=1, source_target_pairs={{0,2},{1,3},{2,0},{3,1},{4,6},{5,7},{6,4},{7,5},{8,10},{9,11},{10,... | collective-permute-start | bytes 294920 | tf_op jit(solution)/shard_map/ppermute | solution.py:404
  134.7 5.2 %collective-permute-start.58 = (bf16[16,3072]{1,0:T(8,128)(2,1)S(1)}, bf16[16,3072]{1,0:T(8,128)(2,1)S(1)}, u32[]{:S(2)}, u32[]{:S(2)}) collective-permute-start(bf16[16,3072]{1,0:T(8,128)(2,1)S(1)} %collective-permute-done.54.refs_3_), channel_id=1, source_target_pairs={{0,2},{1,3},{2,0},{3,1},{4,6},{5,7},{6,4},{7,5},{8,10},{9,11},{10,... | collective-permute-start | bytes 294920 | tf_op jit(solution)/shard_map/ppermute | solution.py:404
  136.4 5.4 %collective-permute-start.56 = (bf16[16,3072]{1,0:T(8,128)(2,1)S(1)}, bf16[16,3072]{1,0:T(8,128)(2,1)S(1)}, u32[]{:S(2)}, u32[]{:S(2)}) collective-permute-start(bf16[16,3072]{1,0:T(8,128)(2,1)S(1)} %collective-permute-done.52.refs_1_), channel_id=1, source_target_pairs={{0,2},{1,3},{2,0},{3,1},{4,6},{5,7},{6,4},{7,5},{8,10},{9,11},{10,... | collective-permute-start | bytes 294920 | tf_op jit(solution)/shard_map/ppermute | solution.py:404
  138.6 4.6 %collective-permute-start.57 = (bf16[16,3072]{1,0:T(8,128)(2,1)S(1)}, bf16[16,3072]{1,0:T(8,128)(2,1)S(1)}, u32[]{:S(2)}, u32[]{:S(2)}) collective-permute-start(bf16[16,3072]{1,0:T(8,128)(2,1)S(1)} %collective-permute-done.53.refs_2_), channel_id=1, source_target_pairs={{0,2},{1,3},{2,0},{3,1},{4,6},{5,7},{6,4},{7,5},{8,10},{9,11},{10,... | collective-permute-start | bytes 294920 | tf_op jit(solution)/shard_map/ppermute | solution.py:404
  139.9 3.4 %collective-permute-start.63 = (bf16[16,3072]{1,0:T(8,128)(2,1)S(1)}, bf16[16,3072]{1,0:T(8,128)(2,1)S(1)}, u32[]{:S(2)}, u32[]{:S(2)}) collective-permute-start(bf16[16,3072]{1,0:T(8,128)(2,1)S(1)} %collective-permute-done.55.refs_4_), channel_id=1, source_target_pairs={{0,1},{1,0},{2,3},{3,2},{4,5},{5,4},{6,7},{7,6},{8,9},{9,8},{10,11... | collective-permute-start | bytes 294920 | tf_op jit(solution)/shard_map/ppermute | solution.py:404
  139.9 3.9 %collective-permute-start.59 = (bf16[16,3072]{1,0:T(8,128)(2,1)S(1)}, bf16[16,3072]{1,0:T(8,128)(2,1)S(1)}, u32[]{:S(2)}, u32[]{:S(2)}) collective-permute-start(bf16[16,3072]{1,0:T(8,128)(2,1)S(1)} %fusion.4.refs_0_), channel_id=1, source_target_pairs={{0,1},{1,0},{2,3},{3,2},{4,5},{5,4},{6,7},{7,6},{8,9},{9,8},{10,11... | collective-permute-start | bytes 294920 | tf_op jit(solution)/shard_map/ppermute | solution.py:404
  140.4 3.4 %collective-permute-start.60 = (bf16[16,3072]{1,0:T(8,128)(2,1)S(1)}, bf16[16,3072]{1,0:T(8,128)(2,1)S(1)}, u32[]{:S(2)}, u32[]{:S(2)}) collective-permute-start(bf16[16,3072]{1,0:T(8,128)(2,1)S(1)} %collective-permute-done.52.refs_1_), channel_id=1, source_target_pairs={{0,1},{1,0},{2,3},{3,2},{4,5},{5,4},{6,7},{7,6},{8,9},{9,8},{10,11... | collective-permute-start | bytes 294920 | tf_op jit(solution)/shard_map/ppermute | solution.py:404
  141.8 2.4 %collective-permute-start.61 = (bf16[16,3072]{1,0:T(8,128)(2,1)S(1)}, bf16[16,3072]{1,0:T(8,128)(2,1)S(1)}, u32[]{:S(2)}, u32[]{:S(2)}) collective-permute-start(bf16[16,3072]{1,0:T(8,128)(2,1)S(1)} %collective-permute-done.53.refs_2_), channel_id=1, source_target_pairs={{0,1},{1,0},{2,3},{3,2},{4,5},{5,4},{6,7},{7,6},{8,9},{9,8},{10,11... | collective-permute-start | bytes 294920 | tf_op jit(solution)/shard_map/ppermute | solution.py:404
  166.4 4.6 %collective-permute-start.77 = (f32[8,3072]{1,0:T(8,128)S(1)}, f32[8,3072]{1,0:T(8,128)S(1)}, u32[]{:S(2)}, u32[]{:S(2)}) collective-permute-start(f32[8,3072]{1,0:T(8,128)S(1)} %get-tuple-element.192), channel_id=1, source_target_pairs={{0,1},{1,0},{2,3},{3,2},{4,5},{5,4},{6,7},{7,6},{8,9},{9,8},{10,11... | collective-permute-start | bytes 294920 | tf_op jit(solution)/shard_map/ppermute | solution.py:404
  166.8 5.6 %collective-permute-start.70 = (bf16[16,3072]{1,0:T(8,128)(2,1)S(1)}, bf16[16,3072]{1,0:T(8,128)(2,1)S(1)}, u32[]{:S(2)}, u32[]{:S(2)}) collective-permute-start(bf16[16,3072]{1,0:T(8,128)(2,1)S(1)} %get-tuple-element.187), channel_id=1, source_target_pairs={{0,2},{1,3},{2,0},{3,1},{4,6},{5,7},{6,4},{7,5},{8,10},{9,11},{10,... | collective-permute-start | bytes 294920 | tf_op jit(solution)/shard_map/ppermute | solution.py:404
  168.2 6.4 %collective-permute-start.72 = (bf16[16,3072]{1,0:T(8,128)(2,1)S(1)}, bf16[16,3072]{1,0:T(8,128)(2,1)S(1)}, u32[]{:S(2)}, u32[]{:S(2)}) collective-permute-start(bf16[16,3072]{1,0:T(8,128)(2,1)S(1)} %get-tuple-element.189), channel_id=1, source_target_pairs={{0,2},{1,3},{2,0},{3,1},{4,6},{5,7},{6,4},{7,5},{8,10},{9,11},{10,... | collective-permute-start | bytes 294920 | tf_op jit(solution)/shard_map/ppermute | solution.py:404
  168.9 7.7 %collective-permute-start.74 = (bf16[16,3072]{1,0:T(8,128)(2,1)S(1)}, bf16[16,3072]{1,0:T(8,128)(2,1)S(1)}, u32[]{:S(2)}, u32[]{:S(2)}) collective-permute-start(bf16[16,3072]{1,0:T(8,128)(2,1)S(1)} %get-tuple-element.191), channel_id=1, source_target_pairs={{0,2},{1,3},{2,0},{3,1},{4,6},{5,7},{6,4},{7,5},{8,10},{9,11},{10,... | collective-permute-start | bytes 294920 | tf_op jit(solution)/shard_map/ppermute | solution.py:404
  170.2 11.2 %collective-permute-start.69 = (bf16[16,3072]{1,0:T(8,128)(2,1)S(1)}, bf16[16,3072]{1,0:T(8,128)(2,1)S(1)}, u32[]{:S(2)}, u32[]{:S(2)}) collective-permute-start(bf16[16,3072]{1,0:T(8,128)(2,1)S(1)} %get-tuple-element.185), channel_id=1, source_target_pairs={{0,2},{1,3},{2,0},{3,1},{4,6},{5,7},{6,4},{7,5},{8,10},{9,11},{10,... | collective-permute-start | bytes 294920 | tf_op jit(solution)/shard_map/ppermute | solution.py:404
  171.0 9.1 %collective-permute-start.78 = (f32[8,3072]{1,0:T(8,128)S(1)}, f32[8,3072]{1,0:T(8,128)S(1)}, u32[]{:S(2)}, u32[]{:S(2)}) collective-permute-start(f32[8,3072]{1,0:T(8,128)S(1)} %add.240), channel_id=1, source_target_pairs={{0,2},{1,3},{2,0},{3,1},{4,6},{5,7},{6,4},{7,5},{8,10},{9,11},{10,... | collective-permute-start | bytes 294920 | tf_op jit(solution)/shard_map/ppermute | solution.py:404
  172.5 10.5 %collective-permute-start.71 = (bf16[16,3072]{1,0:T(8,128)(2,1)S(1)}, bf16[16,3072]{1,0:T(8,128)(2,1)S(1)}, u32[]{:S(2)}, u32[]{:S(2)}) collective-permute-start(bf16[16,3072]{1,0:T(8,128)(2,1)S(1)} %add_convert_fusion.3), channel_id=1, source_target_pairs={{0,12},{4,0},{8,4},{12,8},{1,13},{5,1},{9,5},{13,9},{2,14},{6,2},{... | collective-permute-start | bytes 294920 | tf_op jit(solution)/shard_map/ppermute | solution.py:404
  174.6 9.5 %collective-permute-start.73 = (bf16[16,3072]{1,0:T(8,128)(2,1)S(1)}, bf16[16,3072]{1,0:T(8,128)(2,1)S(1)}, u32[]{:S(2)}, u32[]{:S(2)}) collective-permute-start(bf16[16,3072]{1,0:T(8,128)(2,1)S(1)} %add_convert_fusion.2), channel_id=1, source_target_pairs={{0,8},{4,12},{8,0},{12,4},{1,9},{5,13},{9,1},{13,5},{2,10},{6,14},... | collective-permute-start | bytes 294920 | tf_op jit(solution)/shard_map/ppermute | solution.py:404
  176.7 8.7 %collective-permute-start.75 = (bf16[16,3072]{1,0:T(8,128)(2,1)S(1)}, bf16[16,3072]{1,0:T(8,128)(2,1)S(1)}, u32[]{:S(2)}, u32[]{:S(2)}) collective-permute-start(bf16[16,3072]{1,0:T(8,128)(2,1)S(1)} %add_convert_fusion.1), channel_id=1, source_target_pairs={{0,4},{4,8},{8,12},{12,0},{1,5},{5,9},{9,13},{13,1},{2,6},{6,10},{... | collective-permute-start | bytes 294920 | tf_op jit(solution)/shard_map/ppermute | solution.py:404
  180.1 5.5 %collective-permute-start.76 = (bf16[16,3072]{1,0:T(8,128)(2,1)S(1)}, bf16[16,3072]{1,0:T(8,128)(2,1)S(1)}, u32[]{:S(2)}, u32[]{:S(2)}) collective-permute-start(bf16[16,3072]{1,0:T(8,128)(2,1)S(1)} %fusion.4.refs_0_), channel_id=1, source_target_pairs={{0,16},{1,17},{2,18},{3,19},{4,20},{5,21},{6,22},{7,23},{8,24},{9,... | collective-permute-start | bytes 294920 | tf_op jit(solution)/shard_map/ppermute | solution.py:404
  181.4 7.7 %collective-permute-start.79 = (f32[8,3072]{1,0:T(8,128)S(1)}, f32[8,3072]{1,0:T(8,128)S(1)}, u32[]{:S(2)}, u32[]{:S(2)}) collective-permute-start(f32[8,3072]{1,0:T(8,128)S(1)} %add.241), channel_id=1, source_target_pairs={{0,4},{4,8},{8,12},{12,0},{1,5},{5,9},{9,13},{13,1},{2,6},{6,10},{... | collective-permute-start | bytes 294920 | tf_op jit(solution)/shard_map/ppermute | solution.py:404
  182.9 8.7 %collective-permute-start.80 = (f32[8,3072]{1,0:T(8,128)S(1)}, f32[8,3072]{1,0:T(8,128)S(1)}, u32[]{:S(2)}, u32[]{:S(2)}) collective-permute-start(f32[8,3072]{1,0:T(8,128)S(1)} %add.241), channel_id=1, source_target_pairs={{0,8},{4,12},{8,0},{12,4},{1,9},{5,13},{9,1},{13,5},{2,10},{6,14},... | collective-permute-start | bytes 294920 | tf_op jit(solution)/shard_map/ppermute | solution.py:404
  184.1 7.5 %collective-permute-start.81 = (f32[8,3072]{1,0:T(8,128)S(1)}, f32[8,3072]{1,0:T(8,128)S(1)}, u32[]{:S(2)}, u32[]{:S(2)}) collective-permute-start(f32[8,3072]{1,0:T(8,128)S(1)} %add.241), channel_id=1, source_target_pairs={{0,12},{4,0},{8,4},{12,8},{1,13},{5,1},{9,5},{13,9},{2,14},{6,2},{... | collective-permute-start | bytes 294920 | tf_op jit(solution)/shard_map/ppermute | solution.py:404
  (22 other events, 91.9 us)
where the time goes:
time: 193 us; the launch traced here: 192 us
  starting transfers between devices  71.1 us (37%)
  waiting for transfers between devices  61.4 us (32%)
  Pallas kernels  52.2 us (27%)
  other arithmetic  6.27 us (3%)
    ppermute x82, starting transfers between devices, moved(): return lax.ppermute(block, axes, pairs)  71.1 us
    ppermute x82, waiting for transfers between devices, moved(): return lax.ppermute(block, axes, pairs)  61.4 us
    pallas_call x3, Pallas kernels, expert_call(): pl.pallas_call(functools.partial(with_pieces, body, len(pieces), len(in_s...  52.2 us
  transfers between devices with their start and end apart: 82, of which 46 were waited for; matrix products, arithmetic and copies ran while one was open for 2% of the time, Pallas kernels for 0%

commit v1 on v0

--- a/solution.py
+++ b/solution.py
@@ -57,14 +57,9 @@
     return jnp.where(first != second, both, 0.0)
 
 
-def norm_and_gap(rows_ref, router_ref, signs, hidden_ref):
+def norm_and_gap(rows_ref, squares, router_ref, signs, hidden_ref):
     rows, width = rows_ref.shape
 
-    def square(i, part, total):
-        values = rows_ref[:, part].astype(F32)
-        return total + jnp.sum(values * values, axis=1, keepdims=True)
-
-    squares = tiles(width, square, jnp.zeros((rows, 1), F32))
     inv_rms = lax.rsqrt(squares / width + EPSILON)
 
     def scale(i, part, total):
@@ -114,11 +109,12 @@
 
 
 def select(pick_ref, x_ref, rows_ref):
-    def body(i, part, carry):
-        rows_ref[:, part] = dot_nn(pick_ref[...], x_ref[:, part]).astype(BF16)
-        return carry
-
-    tiles(rows_ref.shape[1], body)
+    def body(i, part, total):
+        rows = dot_nn(pick_ref[...], x_ref[:, part])
+        rows_ref[:, part] = rows.astype(BF16)
+        return total + jnp.sum(rows * rows, axis=1, keepdims=True)
+
+    return tiles(rows_ref.shape[1], body, jnp.zeros((rows_ref.shape[0], 1), F32))
 
 
 def piece_copies(x_refs, x_ref, sems):
@@ -236,12 +232,12 @@
     me = lax.axis_index("expert").astype(F32)
     tail = x_ref[:, width:]
     place_rows(tail.astype(F32), me, place_ref, pick_ref)
-    select(pick_ref, x_ref, rows_ref)
+    squares = select(pick_ref, x_ref, rows_ref)
     info_ref[0] = signs_of(dot_nn(pick_ref[...], tail), me)
 
     @pl.when(section == 0)
     def _():
-        gap = norm_and_gap(rows_ref, router_ref, info_ref[0], hidden_ref)
+        gap = norm_and_gap(rows_ref, squares, router_ref, info_ref[0], hidden_ref)
         info_ref[1] = jnp.broadcast_to(gap, info_ref.shape[1:])
 
         def body(i, part, carry):
@@ -295,9 +291,9 @@
         start_all(gate_loads, up_loads)
         for copy in fetches:
             copy.wait()
-        select(pick_ref, x_ref, rows_ref)
+        squares = select(pick_ref, x_ref, rows_ref)
         signs = info_ref[0]
-        gap = norm_and_gap(rows_ref, router_ref, signs, hidden_ref)
+        gap = norm_and_gap(rows_ref, squares, router_ref, signs, hidden_ref)
         prob = jax.nn.sigmoid(gap)
         prob_ref[...] = jnp.broadcast_to(prob, prob_ref.shape)
         dprob_ref[...] = jnp.zeros_like(dprob_ref)
@@ -445,19 +441,22 @@
             [add(kept, flipped(sent, bit)) for kept, sent in zip(*pair)]
             for pair in zip(groups[:half], groups[half:])
         ]
+    if late is not None:
+        for bit in flips()[:-1]:
+            late = late + flipped(late, bit)
     total = 0.0
     for k, part in enumerate(groups[0]):
         if hop:
             part = moved(part, ("section", "expert"), lambda s, e, k=k: (s + hop, (e - k) % count))
         elif k:
             part = moved(part, ("expert",), lambda e, k=k: ((e - k) % count,))
+        if late is not None and k == count - 2:
+            late = lax.optimization_barrier((part, late))[1]
         total = total + part.astype(F32)
     return total, late
 
 
 def summed(block):
-    for bit in reversed(flips()):
-        block = block + flipped(block, bit)
     count = lax.axis_size("expert")
     total = block
     for k in range(1, count):
@@ -497,7 +496,6 @@
     gain_row = norm_gain[0].astype(F32)
     blank = jnp.zeros((LANES - 1 - experts, width), BF16)
     router_w = jnp.concatenate([router[0].T, blank, norm_gain], axis=0)
-    kept = -(-experts // 8) * 8
     shape = jax.ShapeDtypeStruct
     dot_flops = 2 * rows * width * hidden_units
     row_block, lane_block = pltpu.VMEM((rows, width), BF16), pltpu.VMEM((rows, LANES), F32)
@@ -523,7 +521,7 @@
     back, active, prob, rg, gate_t, up_t = expert_call(
         middle_kernel, pieces,
         [router_w, place, pick, info, stash_a], weights,
-        [shape((rows, hidden_units), BF16), shape((rows, LANES), F32), shape((kept, width), F32)],
+        [shape((rows, hidden_units), BF16), shape((rows, LANES), F32), shape((experts, width), F32)],
         [row_block, row_block, d_block, d_block, lane_block,
          pltpu.SemaphoreType.DMA((hidden_units // tile_of(hidden_units, 512),))],
         4 * dot_flops, far=[shape((hidden_units, width), BF16)] * 2,
@@ -534,13 +532,13 @@
         last_kernel, gathered(grads_mid),
         [router_w, place, pick, info, hidden, prob, rg, stash_a, stash_b, active],
         (gate_t, up_t, weights[2]),
-        [shape((kept, width), F32)],
+        [shape((experts, width), F32)],
         [row_block, d_block, d_block, lane_block],
         3 * dot_flops, by_rows=True,
     )
     grads_end = across(grads_mid, 1)
-    total, rg = combined(out, late=rg)
-    router_total = summed(rg)[:experts].T
+    total, rg = combined(out, late=rg + flipped(rg, flips()[-1]))
+    router_total = summed(rg).T
     grads_start = input_grad(mine, grads_mid, total, gain_row)
     acts_end = (acts_mid.astype(F32) + total).astype(BF16)
     acts = jnp.where(at_start, acts_start, acts_end).reshape(1, micro, toks, width)

time: 193 us -> 189 us (0.979)
  waiting for transfers between devices: 61.4 us -> 56.5 us
    ppermute x82, waiting for transfers between devices: 61.4 us -> 56.5 us  [moved(): return lax.ppermute(block, axes, pairs)]
where the time goes in v1:
time: 189 us; the launch traced here: 188 us
  starting transfers between devices  71.9 us (38%)
  waiting for transfers between devices  56.5 us (30%)
  Pallas kernels  52.1 us (28%)
  other arithmetic  6.26 us (3%)
    ppermute x82, starting transfers between devices, moved(): return lax.ppermute(block, axes, pairs)  71.9 us
    ppermute x82, waiting for transfers between devices, moved(): return lax.ppermute(block, axes, pairs)  56.5 us
    pallas_call x3, Pallas kernels, expert_call(): pl.pallas_call(functools.partial(with_pieces, body, len(pieces), len(in_s...  52.1 us
  transfers between devices with their start and end apart: 82, of which 46 were waited for; matrix products, arithmetic and copies ran while one was open for 2% of the time, Pallas kernels for 0%

profile of v1, /device:TPU:0, one launch (start us, length us, event | category | flops | bytes accessed | tf_op | source)
XLA Modules:
  0.0 188.2 jit_solution(4773202027565579078)
XLA Ops:
  1.4 0.9 fusion.18
  2.4 5.1 %collective-permute-start.2 = (bf16[16,3200]{1,0:T(8,128)(2,1)S(1)}, bf16[16,3200]{1,0:T(8,128)(2,1)S(1)}, u32[]{:S(2)}, u32[]{:S(2)}) collective-permute-start(bf16[16,3200]{1,0:T(8,128)(2,1)S(1)} %fusion.13.refs_0_), channel_id=1, source_target_pairs={{0,12},{4,0},{8,4},{12,8},{1,13},{5,1},{9,5},{13,9},{2,14},{6,2},{... | collective-permute-start | bytes 307208 | tf_op jit(solution)/shard_map/ppermute | solution.py:400
  8.2 1.6 collective-permute-start.15
  9.8 1.0 collective-permute-start.1
  10.8 1.5 collective-permute-start.3
  12.8 4.0 %collective-permute-done.refs_1_ = bf16[16,3200]{1,0:T(8,128)(2,1)S(1)} collective-permute-done((bf16[16,3200]{1,0:T(8,128)(2,1)S(1)}, bf16[16,3200]{1,0:T(8,128)(2,1)S(1)}, u32[]{:S(2)}, u32[]{:S(2)}) %collective-permute-start) | collective-permute-done | bytes 102432 | tf_op jit(solution)/shard_map/ppermute | solution.py:400
  16.8 1.5 collective-permute-start.4
  19.1 1.5 collective-permute-start.5
  21.3 1.0 collective-permute-done.4.refs_5_
  22.3 1.5 collective-permute-done.5.refs_6_
  24.8 0.9 pad_maximum_fusion.refs_16_
  25.8 16.9 %shard_map.103 = (bf16[64,3072]{1,0:T(8,128)(2,1)S(1)}, bf16[64,3072]{1,0:T(8,128)(2,1)S(1)}, bf16[64,3072]{1,0:T(8,128)(2,1)S(1)}, bf16[64,3072]{1,0:T(8,128)(2...) custom-call(bf16[16,3200]{1,0:T(8,128)(2,1)S(1)} %fusion.13.refs_0_,, ...), custom_call_target="tpu_custom_call" | custom-call | flops 7247757312 | bytes 37748736 | tf_op jit(solution)/shard_map/pallas_call | solution.py:379
  43.3 1.2 collective-permute-done.17
  45.1 1.6 collective-permute-start.18
  47.2 1.5 collective-permute-start.22
  49.3 1.6 collective-permute-done.18
  50.9 1.3 collective-permute-start.19
  53.0 1.3 collective-permute-start.21
  55.1 1.3 collective-permute-start.23
  56.5 1.3 collective-permute-start.25
  57.9 1.5 collective-permute-done.23
  59.4 1.3 collective-permute-done.25
  60.7 1.5 collective-permute-start.28
  62.3 2.6 %collective-permute-start.26 = (bf16[16,3072]{1,0:T(8,128)(2,1)S(1)}, bf16[16,3072]{1,0:T(8,128)(2,1)S(1)}, u32[]{:S(2)}, u32[]{:S(2)}) collective-permute-start(bf16[16,3072]{1,0:T(8,128)(2,1)S(1)} %fusion.2.refs_0_), channel_id=1, source_target_pairs={{0,4},{4,8},{8,12},{12,0},{1,5},{5,9},{9,13},{13,1},{2,6},{6,10},{... | collective-permute-start | bytes 294920 | tf_op jit(solution)/shard_map/ppermute | solution.py:400
  64.8 1.4 collective-permute-start.27
  66.5 2.9 %collective-permute-done.28.refs_3_ = bf16[16,3072]{1,0:T(8,128)(2,1)S(1)} collective-permute-done((bf16[16,3072]{1,0:T(8,128)(2,1)S(1)}, bf16[16,3072]{1,0:T(8,128)(2,1)S(1)}, u32[]{:S(2)}, u32[]{:S(2)}) %collective-permute-start.28) | collective-permute-done | bytes 98336 | tf_op jit(solution)/shard_map/ppermute | solution.py:400
  69.4 1.3 collective-permute-start.41
  70.7 2.1 %collective-permute-start.30 = (bf16[16,3072]{1,0:T(8,128)(2,1)S(1)}, bf16[16,3072]{1,0:T(8,128)(2,1)S(1)}, u32[]{:S(2)}, u32[]{:S(2)}) collective-permute-start(bf16[16,3072]{1,0:T(8,128)(2,1)S(1)} %collective-permute-done.26.refs_1_), channel_id=1, source_target_pairs={{0,2},{1,3},{2,0},{3,1},{4,6},{5,7},{6,4},{7,5},{8,10},{9,11},{10,... | collective-permute-start | bytes 294920 | tf_op jit(solution)/shard_map/ppermute | solution.py:400
  73.5 1.2 collective-permute-start.31
  75.2 0.9 collective-permute-done.41
  76.7 1.4 collective-permute-done.31.refs_6_
  80.1 16.5 %shard_map.104 = (bf16[64,3072]{1,0:T(8,128)(2,1)S(1)}, bf16[64,3072]{1,0:T(8,128)(2,1)S(1)}, bf16[64,3072]{1,0:T(8,128)(2,1)S(1)}, bf16[64,3072]{1,0:T(8,128)(2...) custom-call(bf16[16,3072]{1,0:T(8,128)(2,1)S(1)} %fusion.2.refs_0_, ...), custom_call_target="tpu_custom_call" | custom-call | flops 9663676416 | bytes 37748736 | tf_op jit(solution)/shard_map/pallas_call | solution.py:379
  97.2 1.2 collective-permute-done.43
  99.0 1.3 collective-permute-start.44
  100.3 0.8 collective-permute-start.46
  101.1 1.2 collective-permute-start.48
  103.2 1.6 collective-permute-done.44
  104.7 1.3 collective-permute-start.45
  106.9 1.3 collective-permute-start.47
  109.0 1.3 collective-permute-start.49
  110.5 1.3 collective-permute-start.51
  111.8 5.6 %collective-permute-done.45 = bf16[16,3072]{1,0:T(8,128)(2,1)S(1)} collective-permute-done((bf16[16,3072]{1,0:T(8,128)(2,1)S(1)}, bf16[16,3072]{1,0:T(8,128)(2,1)S(1)}, u32[]{:S(2)}, u32[]{:S(2)}) %collective-permute-start.45) | collective-permute-done | bytes 98336 | tf_op jit(solution)/shard_map/ppermute | solution.py:400
  117.4 4.9 %collective-permute-done.47 = bf16[16,3072]{1,0:T(8,128)(2,1)S(1)} collective-permute-done((bf16[16,3072]{1,0:T(8,128)(2,1)S(1)}, bf16[16,3072]{1,0:T(8,128)(2,1)S(1)}, u32[]{:S(2)}, u32[]{:S(2)}) %collective-permute-start.47) | collective-permute-done | bytes 98336 | tf_op jit(solution)/shard_map/ppermute | solution.py:400
  122.3 5.2 %collective-permute-done.49 = bf16[16,3072]{1,0:T(8,128)(2,1)S(1)} collective-permute-done((bf16[16,3072]{1,0:T(8,128)(2,1)S(1)}, bf16[16,3072]{1,0:T(8,128)(2,1)S(1)}, u32[]{:S(2)}, u32[]{:S(2)}) %collective-permute-start.49) | collective-permute-done | bytes 98336 | tf_op jit(solution)/shard_map/ppermute | solution.py:400
  128.7 1.3 collective-permute-start.52
  129.9 1.7 collective-permute-start.53
  131.7 1.3 collective-permute-start.55
  132.9 1.2 collective-permute-done.54.refs_3_
  134.6 1.6 collective-permute-done.52.refs_1_
  136.9 1.6 collective-permute-done.53.refs_2_
  138.6 1.3 collective-permute-start.57
  140.4 0.9 collective-permute-done.56.refs_5_
  141.3 1.9 collective-permute-done.57.refs_6_
  145.2 18.8 %shard_map.105 = (bf16[64,3072]{1,0:T(8,128)(2,1)S(1)}, bf16[64,3072]{1,0:T(8,128)(2,1)S(1)}, bf16[64,3072]{1,0:T(8,128)(2,1)S(1)}, bf16[64,3072]{1,0:T(8,128)(2,1)S(1)}, f32[4,3072]{1,0:T(4,128)S(1)}) custom-call(bf16[16,3072]{1,0:T(8,128)(2,1)S(1)} %fusion.4.refs_0_, bf16[16,3072]{1,0:T(8,128)(2,1)S(1)} %collective-permute-done.52.refs_1_, ...), custom_call_target="tpu_custom_call" | custom-call | flops 7247757312 | bytes 37748736 | tf_op jit(solution)/shard_map/pallas_call | solution.py:379
  166.5 1.3 collective-permute-start.73
  168.7 1.3 collective-permute-start.71
  170.7 1.3 collective-permute-start.70
  172.2 1.0 collective-permute-start.74
  173.2 2.1 %collective-permute-done.71 = bf16[16,3072]{1,0:T(8,128)(2,1)S(1)} collective-permute-done((bf16[16,3072]{1,0:T(8,128)(2,1)S(1)}, bf16[16,3072]{1,0:T(8,128)(2,1)S(1)}, u32[]{:S(2)}, u32[]{:S(2)}) %collective-permute-start.71) | collective-permute-done | bytes 98336 | tf_op jit(solution)/shard_map/ppermute | solution.py:400
  175.3 2.0 %collective-permute-start.72 = (bf16[16,3072]{1,0:T(8,128)(2,1)S(1)}, bf16[16,3072]{1,0:T(8,128)(2,1)S(1)}, u32[]{:S(2)}, u32[]{:S(2)}) collective-permute-start(bf16[16,3072]{1,0:T(8,128)(2,1)S(1)} %add_convert_fusion.3), channel_id=1, source_target_pairs={{0,12},{4,0},{8,4},{12,8},{1,13},{5,1},{9,5},{13,9},{2,14},{6,2},{... | collective-permute-start | bytes 294920 | tf_op jit(solution)/shard_map/ppermute | solution.py:400
  177.4 1.6 collective-permute-start.76
  179.1 1.3 collective-permute-start.77
  180.5 2.8 %collective-permute-start.80 = (f32[4,3072]{1,0:T(4,128)S(1)}, f32[4,3072]{1,0:T(4,128)S(1)}, u32[]{:S(2)}, u32[]{:S(2)}) collective-permute-start(f32[4,3072]{1,0:T(4,128)S(1)} %add.241), channel_id=1, source_target_pairs={{0,8},{4,12},{8,0},{12,4},{1,9},{5,13},{9,1},{13,5},{2,10},{6,14},... | collective-permute-start | bytes 147464 | tf_op jit(solution)/shard_map/ppermute | solution.py:400
  183.3 1.4 collective-permute-start.81
  (152 shorter events, 29.4 us)
Async XLA Ops:
  2.4 9.9 %collective-permute-start.2 = (bf16[16,3200]{1,0:T(8,128)(2,1)S(1)}, bf16[16,3200]{1,0:T(8,128)(2,1)S(1)}, u32[]{:S(2)}, u32[]{:S(2)}) collective-permute-start(bf16[16,3200]{1,0:T(8,128)(2,1)S(1)} %fusion.13.refs_0_), channel_id=1, source_target_pairs={{0,12},{4,0},{8,4},{12,8},{1,13},{5,1},{9,5},{13,9},{2,14},{6,2},{... | collective-permute-start | bytes 307208 | tf_op jit(solution)/shard_map/ppermute | solution.py:400
  8.2 13.0 %collective-permute-start.15 = (bf16[24,3072]{1,0:T(8,128)(2,1)S(1)}, bf16[24,3072]{1,0:T(8,128)(2,1)S(1)}, u32[]{:S(2)}, u32[]{:S(2)}) collective-permute-start(bf16[24,3072]{1,0:T(8,128)(2,1)S(1)} %fusion.12), channel_id=1, source_target_pairs={{0,16},{16,0},{1,17},{17,1},{2,18},{18,2},{3,19},{19,3},{4,20},{20... | collective-permute-start | bytes 442376 | tf_op jit(solution)/shard_map/ppermute | solution.py:400
  9.8 7.1 %collective-permute-start = (bf16[16,3200]{1,0:T(8,128)(2,1)S(1)}, bf16[16,3200]{1,0:T(8,128)(2,1)S(1)}, u32[]{:S(2)}, u32[]{:S(2)}) collective-permute-start(bf16[16,3200]{1,0:T(8,128)(2,1)S(1)} %fusion.13.refs_0_), channel_id=1, source_target_pairs={{0,4},{4,8},{8,12},{12,0},{1,5},{5,9},{9,13},{13,1},{2,6},{6,10},{... | collective-permute-start | bytes 307208 | tf_op jit(solution)/shard_map/ppermute | solution.py:400
  9.8 9.4 %collective-permute-start.1 = (bf16[16,3200]{1,0:T(8,128)(2,1)S(1)}, bf16[16,3200]{1,0:T(8,128)(2,1)S(1)}, u32[]{:S(2)}, u32[]{:S(2)}) collective-permute-start(bf16[16,3200]{1,0:T(8,128)(2,1)S(1)} %fusion.13.refs_0_), channel_id=1, source_target_pairs={{0,8},{4,12},{8,0},{12,4},{1,9},{5,13},{9,1},{13,5},{2,10},{6,14},... | collective-permute-start | bytes 307208 | tf_op jit(solution)/shard_map/ppermute | solution.py:400
  10.8 9.8 %collective-permute-start.3 = (bf16[16,3200]{1,0:T(8,128)(2,1)S(1)}, bf16[16,3200]{1,0:T(8,128)(2,1)S(1)}, u32[]{:S(2)}, u32[]{:S(2)}) collective-permute-start(bf16[16,3200]{1,0:T(8,128)(2,1)S(1)} %fusion.13.refs_0_), channel_id=1, source_target_pairs={{0,2},{1,3},{2,0},{3,1},{4,6},{5,7},{6,4},{7,5},{8,10},{9,11},{10,... | collective-permute-start | bytes 307208 | tf_op jit(solution)/shard_map/ppermute | solution.py:400
  12.3 8.3 %collective-permute-start.6 = (bf16[16,3200]{1,0:T(8,128)(2,1)S(1)}, bf16[16,3200]{1,0:T(8,128)(2,1)S(1)}, u32[]{:S(2)}, u32[]{:S(2)}) collective-permute-start(bf16[16,3200]{1,0:T(8,128)(2,1)S(1)} %collective-permute-done.2.refs_3_), channel_id=1, source_target_pairs={{0,2},{1,3},{2,0},{3,1},{4,6},{5,7},{6,4},{7,5},{8,10},{9,11},{10,... | collective-permute-start | bytes 307208 | tf_op jit(solution)/shard_map/ppermute | solution.py:400
  16.8 5.5 %collective-permute-start.4 = (bf16[16,3200]{1,0:T(8,128)(2,1)S(1)}, bf16[16,3200]{1,0:T(8,128)(2,1)S(1)}, u32[]{:S(2)}, u32[]{:S(2)}) collective-permute-start(bf16[16,3200]{1,0:T(8,128)(2,1)S(1)} %collective-permute-done.refs_1_), channel_id=1, source_target_pairs={{0,2},{1,3},{2,0},{3,1},{4,6},{5,7},{6,4},{7,5},{8,10},{9,11},{10,... | collective-permute-start | bytes 307208 | tf_op jit(solution)/shard_map/ppermute | solution.py:400
  19.1 4.7 %collective-permute-start.5 = (bf16[16,3200]{1,0:T(8,128)(2,1)S(1)}, bf16[16,3200]{1,0:T(8,128)(2,1)S(1)}, u32[]{:S(2)}, u32[]{:S(2)}) collective-permute-start(bf16[16,3200]{1,0:T(8,128)(2,1)S(1)} %collective-permute-done.1.refs_2_), channel_id=1, source_target_pairs={{0,2},{1,3},{2,0},{3,1},{4,6},{5,7},{6,4},{7,5},{8,10},{9,11},{10,... | collective-permute-start | bytes 307208 | tf_op jit(solution)/shard_map/ppermute | solution.py:400
  20.6 3.2 %collective-permute-start.11 = (bf16[16,3200]{1,0:T(8,128)(2,1)S(1)}, bf16[16,3200]{1,0:T(8,128)(2,1)S(1)}, u32[]{:S(2)}, u32[]{:S(2)}) collective-permute-start(bf16[16,3200]{1,0:T(8,128)(2,1)S(1)} %collective-permute-done.3.refs_4_), channel_id=1, source_target_pairs={{0,1},{1,0},{2,3},{3,2},{4,5},{5,4},{6,7},{7,6},{8,9},{9,8},{10,11... | collective-permute-start | bytes 307208 | tf_op jit(solution)/shard_map/ppermute | solution.py:400
  20.6 3.7 %collective-permute-start.10 = (bf16[16,3200]{1,0:T(8,128)(2,1)S(1)}, bf16[16,3200]{1,0:T(8,128)(2,1)S(1)}, u32[]{:S(2)}, u32[]{:S(2)}) collective-permute-start(bf16[16,3200]{1,0:T(8,128)(2,1)S(1)} %collective-permute-done.2.refs_3_), channel_id=1, source_target_pairs={{0,1},{1,0},{2,3},{3,2},{4,5},{5,4},{6,7},{7,6},{8,9},{9,8},{10,11... | collective-permute-start | bytes 307208 | tf_op jit(solution)/shard_map/ppermute | solution.py:400
  21.1 3.2 %collective-permute-start.7 = (bf16[16,3200]{1,0:T(8,128)(2,1)S(1)}, bf16[16,3200]{1,0:T(8,128)(2,1)S(1)}, u32[]{:S(2)}, u32[]{:S(2)}) collective-permute-start(bf16[16,3200]{1,0:T(8,128)(2,1)S(1)} %fusion.13.refs_0_), channel_id=1, source_target_pairs={{0,1},{1,0},{2,3},{3,2},{4,5},{5,4},{6,7},{7,6},{8,9},{9,8},{10,11... | collective-permute-start | bytes 307208 | tf_op jit(solution)/shard_map/ppermute | solution.py:400
  22.3 3.4 %collective-permute-start.8 = (bf16[16,3200]{1,0:T(8,128)(2,1)S(1)}, bf16[16,3200]{1,0:T(8,128)(2,1)S(1)}, u32[]{:S(2)}, u32[]{:S(2)}) collective-permute-start(bf16[16,3200]{1,0:T(8,128)(2,1)S(1)} %collective-permute-done.refs_1_), channel_id=1, source_target_pairs={{0,1},{1,0},{2,3},{3,2},{4,5},{5,4},{6,7},{7,6},{8,9},{9,8},{10,11... | collective-permute-start | bytes 307208 | tf_op jit(solution)/shard_map/ppermute | solution.py:400
  43.0 2.0 %collective-permute-start.16 = (bf16[64,3072]{1,0:T(8,128)(2,1)S(1)}, bf16[64,3072]{1,0:T(8,128)(2,1)S(1)}, u32[]{:S(2)}, u32[]{:S(2)}) collective-permute-start(bf16[64,3072]{1,0:T(8,128)(2,1)S(1)} %get-tuple-element.121), channel_id=1, source_target_pairs={{0,1},{1,0},{2,3},{3,2},{4,5},{5,4},{6,7},{7,6},{8,9},{9,8},{10,11... | collective-permute-start | bytes 1179656 | tf_op jit(solution)/shard_map/ppermute | solution.py:400
  45.1 5.7 %collective-permute-start.18 = (bf16[16,3072]{1,0:T(8,128)(2,1)S(1)}, bf16[16,3072]{1,0:T(8,128)(2,1)S(1)}, u32[]{:S(2)}, u32[]{:S(2)}) collective-permute-start(bf16[16,3072]{1,0:T(8,128)(2,1)S(1)} %get-tuple-element.125), channel_id=1, source_target_pairs={{0,2},{1,3},{2,0},{3,1},{4,6},{5,7},{6,4},{7,5},{8,10},{9,11},{10,... | collective-permute-start | bytes 294920 | tf_op jit(solution)/shard_map/ppermute | solution.py:400
  46.7 6.2 %collective-permute-start.20 = (bf16[16,3072]{1,0:T(8,128)(2,1)S(1)}, bf16[16,3072]{1,0:T(8,128)(2,1)S(1)}, u32[]{:S(2)}, u32[]{:S(2)}) collective-permute-start(bf16[16,3072]{1,0:T(8,128)(2,1)S(1)} %get-tuple-element.127), channel_id=1, source_target_pairs={{0,2},{1,3},{2,0},{3,1},{4,6},{5,7},{6,4},{7,5},{8,10},{9,11},{10,... | collective-permute-start | bytes 294920 | tf_op jit(solution)/shard_map/ppermute | solution.py:400
  47.2 7.8 %collective-permute-start.22 = (bf16[16,3072]{1,0:T(8,128)(2,1)S(1)}, bf16[16,3072]{1,0:T(8,128)(2,1)S(1)}, u32[]{:S(2)}, u32[]{:S(2)}) collective-permute-start(bf16[16,3072]{1,0:T(8,128)(2,1)S(1)} %get-tuple-element.129), channel_id=1, source_target_pairs={{0,2},{1,3},{2,0},{3,1},{4,6},{5,7},{6,4},{7,5},{8,10},{9,11},{10,... | collective-permute-start | bytes 294920 | tf_op jit(solution)/shard_map/ppermute | solution.py:400
  48.7 7.8 %collective-permute-start.24 = (bf16[16,3072]{1,0:T(8,128)(2,1)S(1)}, bf16[16,3072]{1,0:T(8,128)(2,1)S(1)}, u32[]{:S(2)}, u32[]{:S(2)}) collective-permute-start(bf16[16,3072]{1,0:T(8,128)(2,1)S(1)} %get-tuple-element.131), channel_id=1, source_target_pairs={{0,2},{1,3},{2,0},{3,1},{4,6},{5,7},{6,4},{7,5},{8,10},{9,11},{10,... | collective-permute-start | bytes 294920 | tf_op jit(solution)/shard_map/ppermute | solution.py:400
  50.9 7.0 %collective-permute-start.19 = (bf16[16,3072]{1,0:T(8,128)(2,1)S(1)}, bf16[16,3072]{1,0:T(8,128)(2,1)S(1)}, u32[]{:S(2)}, u32[]{:S(2)}) collective-permute-start(bf16[16,3072]{1,0:T(8,128)(2,1)S(1)} %add_convert_fusion.28), channel_id=1, source_target_pairs={{0,16},{4,20},{8,24},{12,28},{1,17},{5,21},{9,25},{13,29},{2,18},{... | collective-permute-start | bytes 294920 | tf_op jit(solution)/shard_map/ppermute | solution.py:400
  53.0 4.9 %collective-permute-start.21 = (bf16[16,3072]{1,0:T(8,128)(2,1)S(1)}, bf16[16,3072]{1,0:T(8,128)(2,1)S(1)}, u32[]{:S(2)}, u32[]{:S(2)}) collective-permute-start(bf16[16,3072]{1,0:T(8,128)(2,1)S(1)} %add_convert_fusion.27), channel_id=1, source_target_pairs={{0,28},{4,16},{8,20},{12,24},{1,29},{5,17},{9,21},{13,25},{2,30},{... | collective-permute-start | bytes 294920 | tf_op jit(solution)/shard_map/ppermute | solution.py:400
  55.1 4.3 %collective-permute-start.23 = (bf16[16,3072]{1,0:T(8,128)(2,1)S(1)}, bf16[16,3072]{1,0:T(8,128)(2,1)S(1)}, u32[]{:S(2)}, u32[]{:S(2)}) collective-permute-start(bf16[16,3072]{1,0:T(8,128)(2,1)S(1)} %add_convert_fusion.26), channel_id=1, source_target_pairs={{0,24},{4,28},{8,16},{12,20},{1,25},{5,29},{9,17},{13,21},{2,26},{... | collective-permute-start | bytes 294920 | tf_op jit(solution)/shard_map/ppermute | solution.py:400
  56.5 4.1 %collective-permute-start.25 = (bf16[16,3072]{1,0:T(8,128)(2,1)S(1)}, bf16[16,3072]{1,0:T(8,128)(2,1)S(1)}, u32[]{:S(2)}, u32[]{:S(2)}) collective-permute-start(bf16[16,3072]{1,0:T(8,128)(2,1)S(1)} %add_convert_fusion.25), channel_id=1, source_target_pairs={{0,20},{4,24},{8,28},{12,16},{1,21},{5,25},{9,29},{13,17},{2,22},{... | collective-permute-start | bytes 294920 | tf_op jit(solution)/shard_map/ppermute | solution.py:400
  60.7 8.7 %collective-permute-start.28 = (bf16[16,3072]{1,0:T(8,128)(2,1)S(1)}, bf16[16,3072]{1,0:T(8,128)(2,1)S(1)}, u32[]{:S(2)}, u32[]{:S(2)}) collective-permute-start(bf16[16,3072]{1,0:T(8,128)(2,1)S(1)} %fusion.2.refs_0_), channel_id=1, source_target_pairs={{0,12},{4,0},{8,4},{12,8},{1,13},{5,1},{9,5},{13,9},{2,14},{6,2},{... | collective-permute-start | bytes 294920 | tf_op jit(solution)/shard_map/ppermute | solution.py:400
  62.3 8.5 %collective-permute-start.26 = (bf16[16,3072]{1,0:T(8,128)(2,1)S(1)}, bf16[16,3072]{1,0:T(8,128)(2,1)S(1)}, u32[]{:S(2)}, u32[]{:S(2)}) collective-permute-start(bf16[16,3072]{1,0:T(8,128)(2,1)S(1)} %fusion.2.refs_0_), channel_id=1, source_target_pairs={{0,4},{4,8},{8,12},{12,0},{1,5},{5,9},{9,13},{13,1},{2,6},{6,10},{... | collective-permute-start | bytes 294920 | tf_op jit(solution)/shard_map/ppermute | solution.py:400
  64.8 8.7 %collective-permute-start.27 = (bf16[16,3072]{1,0:T(8,128)(2,1)S(1)}, bf16[16,3072]{1,0:T(8,128)(2,1)S(1)}, u32[]{:S(2)}, u32[]{:S(2)}) collective-permute-start(bf16[16,3072]{1,0:T(8,128)(2,1)S(1)} %fusion.2.refs_0_), channel_id=1, source_target_pairs={{0,8},{4,12},{8,0},{12,4},{1,9},{5,13},{9,1},{13,5},{2,10},{6,14},... | collective-permute-start | bytes 294920 | tf_op jit(solution)/shard_map/ppermute | solution.py:400
  66.2 8.5 %collective-permute-start.29 = (bf16[16,3072]{1,0:T(8,128)(2,1)S(1)}, bf16[16,3072]{1,0:T(8,128)(2,1)S(1)}, u32[]{:S(2)}, u32[]{:S(2)}) collective-permute-start(bf16[16,3072]{1,0:T(8,128)(2,1)S(1)} %fusion.2.refs_0_), channel_id=1, source_target_pairs={{0,2},{1,3},{2,0},{3,1},{4,6},{5,7},{6,4},{7,5},{8,10},{9,11},{10,... | collective-permute-start | bytes 294920 | tf_op jit(solution)/shard_map/ppermute | solution.py:400
  69.4 5.3 %collective-permute-start.32 = (bf16[16,3072]{1,0:T(8,128)(2,1)S(1)}, bf16[16,3072]{1,0:T(8,128)(2,1)S(1)}, u32[]{:S(2)}, u32[]{:S(2)}) collective-permute-start(bf16[16,3072]{1,0:T(8,128)(2,1)S(1)} %collective-permute-done.28.refs_3_), channel_id=1, source_target_pairs={{0,2},{1,3},{2,0},{3,1},{4,6},{5,7},{6,4},{7,5},{8,10},{9,11},{10,... | collective-permute-start | bytes 294920 | tf_op jit(solution)/shard_map/ppermute | solution.py:400
  69.4 6.7 %collective-permute-start.41 = (bf16[16,3072]{1,0:T(8,128)(2,1)S(1)}, bf16[16,3072]{1,0:T(8,128)(2,1)S(1)}, u32[]{:S(2)}, u32[]{:S(2)}) collective-permute-start(bf16[16,3072]{1,0:T(8,128)(2,1)S(1)} %fusion.2.refs_0_), channel_id=1, source_target_pairs={{16,0},{17,1},{18,2},{19,3},{20,4},{21,5},{22,6},{23,7},{24,8},{25... | collective-permute-start | bytes 294920 | tf_op jit(solution)/shard_map/ppermute | solution.py:400
  70.7 5.7 %collective-permute-start.30 = (bf16[16,3072]{1,0:T(8,128)(2,1)S(1)}, bf16[16,3072]{1,0:T(8,128)(2,1)S(1)}, u32[]{:S(2)}, u32[]{:S(2)}) collective-permute-start(bf16[16,3072]{1,0:T(8,128)(2,1)S(1)} %collective-permute-done.26.refs_1_), channel_id=1, source_target_pairs={{0,2},{1,3},{2,0},{3,1},{4,6},{5,7},{6,4},{7,5},{8,10},{9,11},{10,... | collective-permute-start | bytes 294920 | tf_op jit(solution)/shard_map/ppermute | solution.py:400
  73.5 4.6 %collective-permute-start.31 = (bf16[16,3072]{1,0:T(8,128)(2,1)S(1)}, bf16[16,3072]{1,0:T(8,128)(2,1)S(1)}, u32[]{:S(2)}, u32[]{:S(2)}) collective-permute-start(bf16[16,3072]{1,0:T(8,128)(2,1)S(1)} %collective-permute-done.27.refs_2_), channel_id=1, source_target_pairs={{0,2},{1,3},{2,0},{3,1},{4,6},{5,7},{6,4},{7,5},{8,10},{9,11},{10,... | collective-permute-start | bytes 294920 | tf_op jit(solution)/shard_map/ppermute | solution.py:400
  74.7 3.4 %collective-permute-start.37 = (bf16[16,3072]{1,0:T(8,128)(2,1)S(1)}, bf16[16,3072]{1,0:T(8,128)(2,1)S(1)}, u32[]{:S(2)}, u32[]{:S(2)}) collective-permute-start(bf16[16,3072]{1,0:T(8,128)(2,1)S(1)} %collective-permute-done.29.refs_4_), channel_id=1, source_target_pairs={{0,1},{1,0},{2,3},{3,2},{4,5},{5,4},{6,7},{7,6},{8,9},{9,8},{10,11... | collective-permute-start | bytes 294920 | tf_op jit(solution)/shard_map/ppermute | solution.py:400
  74.7 3.9 %collective-permute-start.33 = (bf16[16,3072]{1,0:T(8,128)(2,1)S(1)}, bf16[16,3072]{1,0:T(8,128)(2,1)S(1)}, u32[]{:S(2)}, u32[]{:S(2)}) collective-permute-start(bf16[16,3072]{1,0:T(8,128)(2,1)S(1)} %fusion.2.refs_0_), channel_id=1, source_target_pairs={{0,1},{1,0},{2,3},{3,2},{4,5},{5,4},{6,7},{7,6},{8,9},{9,8},{10,11... | collective-permute-start | bytes 294920 | tf_op jit(solution)/shard_map/ppermute | solution.py:400
  76.2 2.5 %collective-permute-start.34 = (bf16[16,3072]{1,0:T(8,128)(2,1)S(1)}, bf16[16,3072]{1,0:T(8,128)(2,1)S(1)}, u32[]{:S(2)}, u32[]{:S(2)}) collective-permute-start(bf16[16,3072]{1,0:T(8,128)(2,1)S(1)} %collective-permute-done.26.refs_1_), channel_id=1, source_target_pairs={{0,1},{1,0},{2,3},{3,2},{4,5},{5,4},{6,7},{7,6},{8,9},{9,8},{10,11... | collective-permute-start | bytes 294920 | tf_op jit(solution)/shard_map/ppermute | solution.py:400
  76.4 2.7 %collective-permute-start.35 = (bf16[16,3072]{1,0:T(8,128)(2,1)S(1)}, bf16[16,3072]{1,0:T(8,128)(2,1)S(1)}, u32[]{:S(2)}, u32[]{:S(2)}) collective-permute-start(bf16[16,3072]{1,0:T(8,128)(2,1)S(1)} %collective-permute-done.27.refs_2_), channel_id=1, source_target_pairs={{0,1},{1,0},{2,3},{3,2},{4,5},{5,4},{6,7},{7,6},{8,9},{9,8},{10,11... | collective-permute-start | bytes 294920 | tf_op jit(solution)/shard_map/ppermute | solution.py:400
  99.0 5.7 %collective-permute-start.44 = (bf16[16,3072]{1,0:T(8,128)(2,1)S(1)}, bf16[16,3072]{1,0:T(8,128)(2,1)S(1)}, u32[]{:S(2)}, u32[]{:S(2)}) collective-permute-start(bf16[16,3072]{1,0:T(8,128)(2,1)S(1)} %get-tuple-element.162), channel_id=1, source_target_pairs={{0,2},{1,3},{2,0},{3,1},{4,6},{5,7},{6,4},{7,5},{8,10},{9,11},{10,... | collective-permute-start | bytes 294920 | tf_op jit(solution)/shard_map/ppermute | solution.py:400
  100.3 6.5 %collective-permute-start.46 = (bf16[16,3072]{1,0:T(8,128)(2,1)S(1)}, bf16[16,3072]{1,0:T(8,128)(2,1)S(1)}, u32[]{:S(2)}, u32[]{:S(2)}) collective-permute-start(bf16[16,3072]{1,0:T(8,128)(2,1)S(1)} %get-tuple-element.164), channel_id=1, source_target_pairs={{0,2},{1,3},{2,0},{3,1},{4,6},{5,7},{6,4},{7,5},{8,10},{9,11},{10,... | collective-permute-start | bytes 294920 | tf_op jit(solution)/shard_map/ppermute | solution.py:400
  101.1 7.8 %collective-permute-start.48 = (bf16[16,3072]{1,0:T(8,128)(2,1)S(1)}, bf16[16,3072]{1,0:T(8,128)(2,1)S(1)}, u32[]{:S(2)}, u32[]{:S(2)}) collective-permute-start(bf16[16,3072]{1,0:T(8,128)(2,1)S(1)} %get-tuple-element.166), channel_id=1, source_target_pairs={{0,2},{1,3},{2,0},{3,1},{4,6},{5,7},{6,4},{7,5},{8,10},{9,11},{10,... | collective-permute-start | bytes 294920 | tf_op jit(solution)/shard_map/ppermute | solution.py:400
  102.3 8.1 %collective-permute-start.50 = (bf16[16,3072]{1,0:T(8,128)(2,1)S(1)}, bf16[16,3072]{1,0:T(8,128)(2,1)S(1)}, u32[]{:S(2)}, u32[]{:S(2)}) collective-permute-start(bf16[16,3072]{1,0:T(8,128)(2,1)S(1)} %get-tuple-element.168), channel_id=1, source_target_pairs={{0,2},{1,3},{2,0},{3,1},{4,6},{5,7},{6,4},{7,5},{8,10},{9,11},{10,... | collective-permute-start | bytes 294920 | tf_op jit(solution)/shard_map/ppermute | solution.py:400
  104.7 12.7 %collective-permute-start.45 = (bf16[16,3072]{1,0:T(8,128)(2,1)S(1)}, bf16[16,3072]{1,0:T(8,128)(2,1)S(1)}, u32[]{:S(2)}, u32[]{:S(2)}) collective-permute-start(bf16[16,3072]{1,0:T(8,128)(2,1)S(1)} %add_convert_fusion.16), channel_id=1, source_target_pairs={{16,0},{20,4},{24,8},{28,12},{17,1},{21,5},{25,9},{29,13},{18,2},{... | collective-permute-start | bytes 294920 | tf_op jit(solution)/shard_map/ppermute | solution.py:400
  106.9 15.4 %collective-permute-start.47 = (bf16[16,3072]{1,0:T(8,128)(2,1)S(1)}, bf16[16,3072]{1,0:T(8,128)(2,1)S(1)}, u32[]{:S(2)}, u32[]{:S(2)}) collective-permute-start(bf16[16,3072]{1,0:T(8,128)(2,1)S(1)} %add_convert_fusion.15), channel_id=1, source_target_pairs={{16,12},{20,0},{24,4},{28,8},{17,13},{21,1},{25,5},{29,9},{18,14},... | collective-permute-start | bytes 294920 | tf_op jit(solution)/shard_map/ppermute | solution.py:400
  109.0 18.5 %collective-permute-start.49 = (bf16[16,3072]{1,0:T(8,128)(2,1)S(1)}, bf16[16,3072]{1,0:T(8,128)(2,1)S(1)}, u32[]{:S(2)}, u32[]{:S(2)}) collective-permute-start(bf16[16,3072]{1,0:T(8,128)(2,1)S(1)} %add_convert_fusion.14), channel_id=1, source_target_pairs={{16,8},{20,12},{24,0},{28,4},{17,9},{21,13},{25,1},{29,5},{18,10},... | collective-permute-start | bytes 294920 | tf_op jit(solution)/shard_map/ppermute | solution.py:400
  110.5 17.0 %collective-permute-start.51 = (bf16[16,3072]{1,0:T(8,128)(2,1)S(1)}, bf16[16,3072]{1,0:T(8,128)(2,1)S(1)}, u32[]{:S(2)}, u32[]{:S(2)}) collective-permute-start(bf16[16,3072]{1,0:T(8,128)(2,1)S(1)} %add_convert_fusion.13), channel_id=1, source_target_pairs={{16,4},{20,8},{24,12},{28,0},{17,5},{21,9},{25,13},{29,1},{18,6},{... | collective-permute-start | bytes 294920 | tf_op jit(solution)/shard_map/ppermute | solution.py:400
  127.9 6.3 %collective-permute-start.54 = (bf16[16,3072]{1,0:T(8,128)(2,1)S(1)}, bf16[16,3072]{1,0:T(8,128)(2,1)S(1)}, u32[]{:S(2)}, u32[]{:S(2)}) collective-permute-start(bf16[16,3072]{1,0:T(8,128)(2,1)S(1)} %fusion.4.refs_0_), channel_id=1, source_target_pairs={{0,12},{4,0},{8,4},{12,8},{1,13},{5,1},{9,5},{13,9},{2,14},{6,2},{... | collective-permute-start | bytes 294920 | tf_op jit(solution)/shard_map/ppermute | solution.py:400
  128.7 7.6 %collective-permute-start.52 = (bf16[16,3072]{1,0:T(8,128)(2,1)S(1)}, bf16[16,3072]{1,0:T(8,128)(2,1)S(1)}, u32[]{:S(2)}, u32[]{:S(2)}) collective-permute-start(bf16[16,3072]{1,0:T(8,128)(2,1)S(1)} %fusion.4.refs_0_), channel_id=1, source_target_pairs={{0,4},{4,8},{8,12},{12,0},{1,5},{5,9},{9,13},{13,1},{2,6},{6,10},{... | collective-permute-start | bytes 294920 | tf_op jit(solution)/shard_map/ppermute | solution.py:400
  129.9 8.6 %collective-permute-start.53 = (bf16[16,3072]{1,0:T(8,128)(2,1)S(1)}, bf16[16,3072]{1,0:T(8,128)(2,1)S(1)}, u32[]{:S(2)}, u32[]{:S(2)}) collective-permute-start(bf16[16,3072]{1,0:T(8,128)(2,1)S(1)} %fusion.4.refs_0_), channel_id=1, source_target_pairs={{0,8},{4,12},{8,0},{12,4},{1,9},{5,13},{9,1},{13,5},{2,10},{6,14},... | collective-permute-start | bytes 294920 | tf_op jit(solution)/shard_map/ppermute | solution.py:400
  131.7 8.2 %collective-permute-start.55 = (bf16[16,3072]{1,0:T(8,128)(2,1)S(1)}, bf16[16,3072]{1,0:T(8,128)(2,1)S(1)}, u32[]{:S(2)}, u32[]{:S(2)}) collective-permute-start(bf16[16,3072]{1,0:T(8,128)(2,1)S(1)} %fusion.4.refs_0_), channel_id=1, source_target_pairs={{0,2},{1,3},{2,0},{3,1},{4,6},{5,7},{6,4},{7,5},{8,10},{9,11},{10,... | collective-permute-start | bytes 294920 | tf_op jit(solution)/shard_map/ppermute | solution.py:400
  134.2 5.7 %collective-permute-start.58 = (bf16[16,3072]{1,0:T(8,128)(2,1)S(1)}, bf16[16,3072]{1,0:T(8,128)(2,1)S(1)}, u32[]{:S(2)}, u32[]{:S(2)}) collective-permute-start(bf16[16,3072]{1,0:T(8,128)(2,1)S(1)} %collective-permute-done.54.refs_3_), channel_id=1, source_target_pairs={{0,2},{1,3},{2,0},{3,1},{4,6},{5,7},{6,4},{7,5},{8,10},{9,11},{10,... | collective-permute-start | bytes 294920 | tf_op jit(solution)/shard_map/ppermute | solution.py:400
  136.3 5.1 %collective-permute-start.56 = (bf16[16,3072]{1,0:T(8,128)(2,1)S(1)}, bf16[16,3072]{1,0:T(8,128)(2,1)S(1)}, u32[]{:S(2)}, u32[]{:S(2)}) collective-permute-start(bf16[16,3072]{1,0:T(8,128)(2,1)S(1)} %collective-permute-done.52.refs_1_), channel_id=1, source_target_pairs={{0,2},{1,3},{2,0},{3,1},{4,6},{5,7},{6,4},{7,5},{8,10},{9,11},{10,... | collective-permute-start | bytes 294920 | tf_op jit(solution)/shard_map/ppermute | solution.py:400
  138.6 4.6 %collective-permute-start.57 = (bf16[16,3072]{1,0:T(8,128)(2,1)S(1)}, bf16[16,3072]{1,0:T(8,128)(2,1)S(1)}, u32[]{:S(2)}, u32[]{:S(2)}) collective-permute-start(bf16[16,3072]{1,0:T(8,128)(2,1)S(1)} %collective-permute-done.53.refs_2_), channel_id=1, source_target_pairs={{0,2},{1,3},{2,0},{3,1},{4,6},{5,7},{6,4},{7,5},{8,10},{9,11},{10,... | collective-permute-start | bytes 294920 | tf_op jit(solution)/shard_map/ppermute | solution.py:400
  139.8 3.4 %collective-permute-start.63 = (bf16[16,3072]{1,0:T(8,128)(2,1)S(1)}, bf16[16,3072]{1,0:T(8,128)(2,1)S(1)}, u32[]{:S(2)}, u32[]{:S(2)}) collective-permute-start(bf16[16,3072]{1,0:T(8,128)(2,1)S(1)} %collective-permute-done.55.refs_4_), channel_id=1, source_target_pairs={{0,1},{1,0},{2,3},{3,2},{4,5},{5,4},{6,7},{7,6},{8,9},{9,8},{10,11... | collective-permute-start | bytes 294920 | tf_op jit(solution)/shard_map/ppermute | solution.py:400
  139.8 3.9 %collective-permute-start.59 = (bf16[16,3072]{1,0:T(8,128)(2,1)S(1)}, bf16[16,3072]{1,0:T(8,128)(2,1)S(1)}, u32[]{:S(2)}, u32[]{:S(2)}) collective-permute-start(bf16[16,3072]{1,0:T(8,128)(2,1)S(1)} %fusion.4.refs_0_), channel_id=1, source_target_pairs={{0,1},{1,0},{2,3},{3,2},{4,5},{5,4},{6,7},{7,6},{8,9},{9,8},{10,11... | collective-permute-start | bytes 294920 | tf_op jit(solution)/shard_map/ppermute | solution.py:400
  140.4 3.4 %collective-permute-start.60 = (bf16[16,3072]{1,0:T(8,128)(2,1)S(1)}, bf16[16,3072]{1,0:T(8,128)(2,1)S(1)}, u32[]{:S(2)}, u32[]{:S(2)}) collective-permute-start(bf16[16,3072]{1,0:T(8,128)(2,1)S(1)} %collective-permute-done.52.refs_1_), channel_id=1, source_target_pairs={{0,1},{1,0},{2,3},{3,2},{4,5},{5,4},{6,7},{7,6},{8,9},{9,8},{10,11... | collective-permute-start | bytes 294920 | tf_op jit(solution)/shard_map/ppermute | solution.py:400
  141.3 2.9 %collective-permute-start.61 = (bf16[16,3072]{1,0:T(8,128)(2,1)S(1)}, bf16[16,3072]{1,0:T(8,128)(2,1)S(1)}, u32[]{:S(2)}, u32[]{:S(2)}) collective-permute-start(bf16[16,3072]{1,0:T(8,128)(2,1)S(1)} %collective-permute-done.53.refs_2_), channel_id=1, source_target_pairs={{0,1},{1,0},{2,3},{3,2},{4,5},{5,4},{6,7},{7,6},{8,9},{9,8},{10,11... | collective-permute-start | bytes 294920 | tf_op jit(solution)/shard_map/ppermute | solution.py:400
  166.5 5.7 %collective-permute-start.73 = (bf16[16,3072]{1,0:T(8,128)(2,1)S(1)}, bf16[16,3072]{1,0:T(8,128)(2,1)S(1)}, u32[]{:S(2)}, u32[]{:S(2)}) collective-permute-start(bf16[16,3072]{1,0:T(8,128)(2,1)S(1)} %get-tuple-element.190), channel_id=1, source_target_pairs={{0,2},{1,3},{2,0},{3,1},{4,6},{5,7},{6,4},{7,5},{8,10},{9,11},{10,... | collective-permute-start | bytes 294920 | tf_op jit(solution)/shard_map/ppermute | solution.py:400
  167.9 11.2 %collective-permute-start.78 = (f32[4,3072]{1,0:T(4,128)S(1)}, f32[4,3072]{1,0:T(4,128)S(1)}, u32[]{:S(2)}, u32[]{:S(2)}) collective-permute-start(f32[4,3072]{1,0:T(4,128)S(1)} %add.230), channel_id=1, source_target_pairs={{0,2},{1,3},{2,0},{3,1},{4,6},{5,7},{6,4},{7,5},{8,10},{9,11},{10,... | collective-permute-start | bytes 147464 | tf_op jit(solution)/shard_map/ppermute | solution.py:400
  168.7 6.7 %collective-permute-start.71 = (bf16[16,3072]{1,0:T(8,128)(2,1)S(1)}, bf16[16,3072]{1,0:T(8,128)(2,1)S(1)}, u32[]{:S(2)}, u32[]{:S(2)}) collective-permute-start(bf16[16,3072]{1,0:T(8,128)(2,1)S(1)} %get-tuple-element.188), channel_id=1, source_target_pairs={{0,2},{1,3},{2,0},{3,1},{4,6},{5,7},{6,4},{7,5},{8,10},{9,11},{10,... | collective-permute-start | bytes 294920 | tf_op jit(solution)/shard_map/ppermute | solution.py:400
  169.9 7.5 %collective-permute-start.75 = (bf16[16,3072]{1,0:T(8,128)(2,1)S(1)}, bf16[16,3072]{1,0:T(8,128)(2,1)S(1)}, u32[]{:S(2)}, u32[]{:S(2)}) collective-permute-start(bf16[16,3072]{1,0:T(8,128)(2,1)S(1)} %get-tuple-element.192), channel_id=1, source_target_pairs={{0,2},{1,3},{2,0},{3,1},{4,6},{5,7},{6,4},{7,5},{8,10},{9,11},{10,... | collective-permute-start | bytes 294920 | tf_op jit(solution)/shard_map/ppermute | solution.py:400
  170.7 9.8 %collective-permute-start.70 = (bf16[16,3072]{1,0:T(8,128)(2,1)S(1)}, bf16[16,3072]{1,0:T(8,128)(2,1)S(1)}, u32[]{:S(2)}, u32[]{:S(2)}) collective-permute-start(bf16[16,3072]{1,0:T(8,128)(2,1)S(1)} %get-tuple-element.186), channel_id=1, source_target_pairs={{0,2},{1,3},{2,0},{3,1},{4,6},{5,7},{6,4},{7,5},{8,10},{9,11},{10,... | collective-permute-start | bytes 294920 | tf_op jit(solution)/shard_map/ppermute | solution.py:400
  172.2 8.2 %collective-permute-start.74 = (bf16[16,3072]{1,0:T(8,128)(2,1)S(1)}, bf16[16,3072]{1,0:T(8,128)(2,1)S(1)}, u32[]{:S(2)}, u32[]{:S(2)}) collective-permute-start(bf16[16,3072]{1,0:T(8,128)(2,1)S(1)} %add_convert_fusion.2), channel_id=1, source_target_pairs={{0,8},{4,12},{8,0},{12,4},{1,9},{5,13},{9,1},{13,5},{2,10},{6,14},... | collective-permute-start | bytes 294920 | tf_op jit(solution)/shard_map/ppermute | solution.py:400
  175.3 8.0 %collective-permute-start.72 = (bf16[16,3072]{1,0:T(8,128)(2,1)S(1)}, bf16[16,3072]{1,0:T(8,128)(2,1)S(1)}, u32[]{:S(2)}, u32[]{:S(2)}) collective-permute-start(bf16[16,3072]{1,0:T(8,128)(2,1)S(1)} %add_convert_fusion.3), channel_id=1, source_target_pairs={{0,12},{4,0},{8,4},{12,8},{1,13},{5,1},{9,5},{13,9},{2,14},{6,2},{... | collective-permute-start | bytes 294920 | tf_op jit(solution)/shard_map/ppermute | solution.py:400
  177.4 7.3 %collective-permute-start.76 = (bf16[16,3072]{1,0:T(8,128)(2,1)S(1)}, bf16[16,3072]{1,0:T(8,128)(2,1)S(1)}, u32[]{:S(2)}, u32[]{:S(2)}) collective-permute-start(bf16[16,3072]{1,0:T(8,128)(2,1)S(1)} %add_convert_fusion.1), channel_id=1, source_target_pairs={{0,4},{4,8},{8,12},{12,0},{1,5},{5,9},{9,13},{13,1},{2,6},{6,10},{... | collective-permute-start | bytes 294920 | tf_op jit(solution)/shard_map/ppermute | solution.py:400
  179.1 5.9 %collective-permute-start.77 = (bf16[16,3072]{1,0:T(8,128)(2,1)S(1)}, bf16[16,3072]{1,0:T(8,128)(2,1)S(1)}, u32[]{:S(2)}, u32[]{:S(2)}) collective-permute-start(bf16[16,3072]{1,0:T(8,128)(2,1)S(1)} %fusion.4.refs_0_), channel_id=1, source_target_pairs={{0,16},{1,17},{2,18},{3,19},{4,20},{5,21},{6,22},{7,23},{8,24},{9,... | collective-permute-start | bytes 294920 | tf_op jit(solution)/shard_map/ppermute | solution.py:400
  180.4 6.0 %collective-permute-start.79 = (f32[4,3072]{1,0:T(4,128)S(1)}, f32[4,3072]{1,0:T(4,128)S(1)}, u32[]{:S(2)}, u32[]{:S(2)}) collective-permute-start(f32[4,3072]{1,0:T(4,128)S(1)} %add.241), channel_id=1, source_target_pairs={{0,4},{4,8},{8,12},{12,0},{1,5},{5,9},{9,13},{13,1},{2,6},{6,10},{... | collective-permute-start | bytes 147464 | tf_op jit(solution)/shard_map/ppermute | solution.py:400
  180.5 6.7 %collective-permute-start.80 = (f32[4,3072]{1,0:T(4,128)S(1)}, f32[4,3072]{1,0:T(4,128)S(1)}, u32[]{:S(2)}, u32[]{:S(2)}) collective-permute-start(f32[4,3072]{1,0:T(4,128)S(1)} %add.241), channel_id=1, source_target_pairs={{0,8},{4,12},{8,0},{12,4},{1,9},{5,13},{9,1},{13,5},{2,10},{6,14},... | collective-permute-start | bytes 147464 | tf_op jit(solution)/shard_map/ppermute | solution.py:400
  183.3 4.2 %collective-permute-start.81 = (f32[4,3072]{1,0:T(4,128)S(1)}, f32[4,3072]{1,0:T(4,128)S(1)}, u32[]{:S(2)}, u32[]{:S(2)}) collective-permute-start(f32[4,3072]{1,0:T(4,128)S(1)} %add.241), channel_id=1, source_target_pairs={{0,12},{4,0},{8,4},{12,8},{1,13},{5,1},{9,5},{13,9},{2,14},{6,2},{... | collective-permute-start | bytes 147464 | tf_op jit(solution)/shard_map/ppermute | solution.py:400
  (22 other events, 92.4 us)
